TPU v7x, 512 devices: a whole 4x8x8 slice. The times are simulated.
512 devices in a mesh: row: 16 (over y_lo, x, core), col: 32 (over z, y_hi).
Axes of the slice: x: 4, y: 8 (y_hi: 4, y_lo: 2; y = y_hi * 2 + y_lo), z: 8, core: 2. Of those that a mesh axis runs over, the one named last changes fastest.
Arguments:
- ginv_top: bfloat16 [8192, 8192], P('col', 'row'), may hold values from -6 to 6
- panel_one: bfloat16 [8192, 2048], P(('row', 'col')), may hold values from -0.09375 to 0.09375
- panel_two: bfloat16 [8192, 4096], P(('row', 'col')), may hold values from -0.125 to 0.125
- parent_link: bfloat16 [2048, 1024], P('row'), may hold values from -0.25 to 0.25
- dinv_one: bfloat16 [512, 2048], P('col', 'row'), may hold values from -6 to 6
- struct_one: int32 [4, 8], replicated, may hold values from 0 to 15, as said below
- struct_two: int32 [8, 4], replicated, may hold values from 0 to 15, as said below
Outputs:
- ginv_one: bfloat16 [8192, 2048], P('col', 'row')
- diag_one: bfloat16 [512, 2048], P('col', 'row')
- ginv_two: bfloat16 [4096, 8192], P('row', 'col')
Inputs may be any that keep to these rules, and one draw needn't show every extreme that they name: `struct_one`: each row lists 8 distinct ancestor block indices in rising order; every row holds 15, and row 0 holds 0. `struct_two`: row q lists 4 distinct indices in rising order, all taken from row q // 2 of struct_one; row 0 holds 0 and row 1 holds 15.
All inputs are finite; a program needn't handle non-finite values.
Results may differ from a plain program's by a relative error of at most 0.02.
Values may be sent and summed in bfloat16 or wider, within the bound.
No kernel may reach another device: no remote copies, remote signals or barrier semaphores. Data moves between devices by JAX's collectives and lax.ppermute only.
A program may use at most 64 MiB of HBM per device.

v0:
```python
import jax
import jax.numpy as jnp
from jax import lax
from jax.sharding import PartitionSpec as P


def spread(value, axis, source):
    kept = jnp.where(lax.axis_index(axis) == source, value, 0).astype(value.dtype)
    return lax.psum(kept, axis)


def grouped_product(wide_left, narrow_right, first_col, block_width, col_mask):
    row_total = wide_left.shape[0]
    slab_width = narrow_right.shape[1]
    groups = max(slab_width // block_width, 1)
    group_width = min(slab_width, block_width)
    first_node = first_col // block_width
    chosen = lax.dynamic_slice_in_dim(wide_left, first_node * block_width, groups * block_width, 1)
    chosen = chosen.reshape(row_total, groups, block_width)
    right_groups = narrow_right.reshape(row_total, groups, group_width)
    result = jnp.einsum("inb,ing->bng", chosen, right_groups, preferred_element_type=jnp.float32)
    weights = lax.dynamic_slice_in_dim(col_mask, first_node, groups, 0)
    result = result * weights[None, :, None]
    return result.reshape(block_width, slab_width)


def per_device(ginv_top, panel_one, panel_two, parent_link, dinv_one, struct_one, struct_two):
    row_count = lax.axis_size("row")
    col_count = lax.axis_size("col")
    row_index = lax.axis_index("row")
    col_index = lax.axis_index("col")
    part_rows = ginv_top.shape[0]
    block_width = ginv_top.shape[1]
    lower_count = struct_two.shape[0]
    col_ratio = col_count // row_count
    member_one = jnp.any(struct_one == row_index, axis=1).astype(jnp.float32)
    member_two = jnp.any(struct_two == row_index, axis=1).astype(jnp.float32)
    mask_one = jnp.repeat(member_one, block_width)
    mask_two = jnp.repeat(member_two, block_width)
    gathered_one = lax.all_gather(panel_one, "col", axis=0, tiled=True)
    partial_one = (
        jnp.dot(ginv_top, gathered_one, preferred_element_type=jnp.float32) * mask_one[None, :]
    )
    sums_one = lax.psum_scatter(
        partial_one.astype(jnp.bfloat16), "row", scatter_dimension=1, tiled=True
    ).astype(jnp.float32)
    ginv_one = (-sums_one).astype(jnp.bfloat16)
    owner_row = col_index // col_ratio
    panel_part = lax.dynamic_slice_in_dim(
        gathered_one, col_index % col_ratio * part_rows, part_rows, 0
    )
    cross_panel = spread(panel_part, "row", owner_row)
    member_cross = jnp.any(struct_one == owner_row, axis=1).astype(jnp.float32)
    slab_width = ginv_one.shape[1]
    diag_part = grouped_product(
        cross_panel, ginv_one, row_index * slab_width, block_width, member_cross
    )
    diag_sums = lax.psum_scatter(
        diag_part.astype(jnp.bfloat16), "col", scatter_dimension=0, tiled=True
    ).astype(jnp.float32)
    diag_one = (dinv_one.astype(jnp.float32) - diag_sums).astype(jnp.bfloat16)
    gathered_two = lax.all_gather(panel_two, "col", axis=0, tiled=True)
    groups = max(slab_width // block_width, 1)
    group_width = min(slab_width, block_width)
    first_parent = row_index * slab_width // block_width
    link_groups = parent_link.reshape(groups, group_width, 2 * block_width)
    upper_groups = ginv_one.reshape(part_rows, groups, group_width)
    parent_terms = jnp.einsum(
        "ngh,ing->nhi", link_groups, upper_groups, preferred_element_type=jnp.float32
    )
    parent_terms = parent_terms.reshape(groups * 2 * block_width, part_rows)
    parent_full = jnp.zeros((lower_count * block_width, part_rows), jnp.float32)
    parent_full = lax.dynamic_update_slice_in_dim(
        parent_full, parent_terms, first_parent * 2 * block_width, 0
    )
    dims = (((0,), (1,)), ((), ()))
    direct = lax.dot_general(gathered_two, ginv_top, dims, preferred_element_type=jnp.float32)
    direct = direct * mask_two[:, None]
    sums_two = lax.psum_scatter(
        (direct + parent_full).astype(jnp.bfloat16), "row", scatter_dimension=0, tiled=True
    ).astype(jnp.float32)
    ginv_two = (-sums_two).astype(jnp.bfloat16)
    return (ginv_one, diag_one, ginv_two)


def solution(mesh):
    return jax.shard_map(
        per_device,
        mesh=mesh,
        in_specs=(
            P("col", "row"),
            P(("row", "col"), None),
            P(("row", "col"), None),
            P("row", None),
            P("col", "row"),
            P(),
            P(),
        ),
        out_specs=(P("col", "row"), P("col", "row"), P("row", "col")),
        check_vma=False,
    )
```

profile of v0, /device:TPU:1, one launch (start us, length us, event | category | flops | bytes accessed | tf_op | source)
XLA Modules:
  0.0 689.0 jit_solution(9300723569310380873)
XLA Ops:
  7.2 0.0 all-gather.3.cloned.1.call-start
  7.2 0.7 all-gather.3.cloned.1.call-update
  7.9 0.0 reduce-scatter.10.cloned.1.call-start
  8.0 0.8 compare_reduce_fusion.1
  8.8 0.1 broadcast_bitcast_fusion.1
  8.9 92.3 %all-gather.3.cloned.1.call-done = bf16[512,2048]{1,0:T(8,128)(2,1)} async-done(((bf16[16,2048]{1,0:T(8,128)(2,1)}), bf16[512,2048]{1,0:T(8,128)(2,1)}) %all-gather.3.cloned.1.call-update) | async-done | bytes 2097168 | tf_op jit(solution)/shard_map/all_gather | solution.py:40
  101.2 2.5 fusion
  103.6 1.3 copy.17
  104.9 0.0 reduce-scatter.10.cloned.1.call-update
  105.0 0.0 all-reduce.2.cloned.1.call-start
  105.0 1.2 dynamic-slice_select_fusion
  106.3 0.0 all-gather.5.cloned.1.call-start
  106.3 0.5 all-gather.5.cloned.1.call-update
  106.9 0.0 reduce-scatter.12.cloned.1.call-start
  107.0 0.1 broadcast_bitcast_fusion
  107.1 0.6 dynamic_slice.11
  107.7 59.4 %reduce-scatter.10.cloned.1.call-done = bf16[128,256]{1,0:T(8,128)(2,1)} async-done(((bf16[2048,256]{1,0:T(8,128)(2,1)}), bf16[128,256]{1,0:T(8,128)(2,1)}) %reduce-scatter.10.cloned.1.call-update) | async-done | bytes 65552
  167.1 0.9 copy.18
  168.1 132.2 %all-reduce.2.cloned.1.call-done = bf16[256,2048]{1,0:T(8,128)(2,1)} async-done(((bf16[256,2048]{1,0:T(8,128)(2,1)}), bf16[256,2048]{1,0:T(8,128)(2,1)}) %all-reduce.2.cloned.1.call-update) | async-done | bytes 1048592 | tf_op jit(solution)/shard_map/psum | solution.py:9
  300.3 1.8 fusion.4
  302.1 0.8 copy.19
  302.9 0.0 reduce-scatter.8.cloned.1.call-start
  303.0 102.3 %all-gather.5.cloned.1.call-done = bf16[512,4096]{1,0:T(8,128)(2,1)} async-done(((bf16[16,4096]{1,0:T(8,128)(2,1)}), bf16[512,4096]{1,0:T(8,128)(2,1)}) %all-gather.5.cloned.1.call-update) | async-done | bytes 4194320 | tf_op jit(solution)/shard_map/all_gather | solution.py:62
  405.3 3.5 convolution_multiply_fusion
  408.8 0.4 fusion.2
  409.2 1.5 convert_element_type.63
  410.7 0.1 copy.13
  410.9 198.9 %reduce-scatter.12.cloned.1.call-done = bf16[16,128]{1,0:T(8,128)(2,1)} async-done(((bf16[512,128]{1,0:T(8,128)(2,1)}), bf16[16,128]{1,0:T(8,128)(2,1)}) %reduce-scatter.12.cloned.1.call-update) | async-done | bytes 4112
  609.8 0.8 copy.20
  610.6 0.7 copy.15
  611.3 69.3 %reduce-scatter.8.cloned.1.call-done = bf16[256,256]{1,0:T(8,128)(2,1)} async-done(((bf16[4096,256]{1,0:T(8,128)(2,1)}), bf16[256,256]{1,0:T(8,128)(2,1)}) %reduce-scatter.8.cloned.1.call-update) | async-done | bytes 131088 | tf_op jit(solution)/shard_map/reduce_scatter | solution.py:79
  680.5 1.6 negate_convert_fusion
  (23 shorter events, 0.2 us)
Async XLA Ops:
  7.2 94.0 %copy-start = (bf16[256,512]{1,0:T(8,128)(2,1)S(1)}, bf16[256,512]{1,0:T(8,128)(2,1)}, u32[]{:S(2)}) copy-start(bf16[256,512]{1,0:T(8,128)(2,1)} %param.7) | copy-start | bytes 786436
  7.2 94.0 %all-gather.3.cloned.1.call-start = ((), (), s32[]{:S(2)}) async-start(), calls=%async_computation.3 | async-start | bytes 2162688 | tf_op jit(solution)/shard_map/all_gather | solution.py:40
  7.9 159.2 %reduce-scatter.10.cloned.1.call-start = ((), (), s32[]{:S(2)}) async-start(), calls=%async_computation.7 | async-start | bytes 1114112
  101.2 3.9 copy-start.1
  101.2 5.8 copy-start.5
  105.0 195.3 %all-reduce.2.cloned.1.call-start = ((), (), s32[]{:S(2)}) async-start(), calls=%async_computation.4 | async-start | bytes 2097152 | tf_op jit(solution)/shard_map/psum | solution.py:9
  106.3 299.0 %all-gather.5.cloned.1.call-start = ((), (), s32[]{:S(2)}) async-start(), calls=%async_computation.5 | async-start | bytes 4325376 | tf_op jit(solution)/shard_map/all_gather | solution.py:62
  106.9 502.9 %reduce-scatter.12.cloned.1.call-start = ((), (), s32[]{:S(2)}) async-start(), calls=%async_computation.8 | async-start | bytes 135168
  168.1 240.7 %copy-start.2 = (bf16[256,128]{1,0:T(8,128)(2,1)}, bf16[256,128]{1,0:T(8,128)(2,1)S(1)}, u32[]{:S(2)}) copy-start(bf16[256,128]{1,0:T(8,128)(2,1)S(1)} %negate_convert_fusion.1) | copy-start | bytes 196612
  302.9 377.6 %reduce-scatter.8.cloned.1.call-start = ((), (), s32[]{:S(2)}) async-start(), calls=%async_computation.6 | async-start | bytes 2228224 | tf_op jit(solution)/shard_map/reduce_scatter | solution.py:79
  405.3 3.5 copy-start.3
  409.2 1.6 copy-start.4
Sparse Core Ops, SparseCore 0:
  11.2 89.9 all-gather.2
  105.1 61.9 reduce-scatter.9
  170.3 129.9 all-reduce.1
  303.3 101.9 all-gather.4
  409.9 199.8 reduce-scatter.11
  612.7 67.7 reduce-scatter.7
where the time goes:
time: 691 us; the launch traced here: 689 us
  waiting for transfers between devices  656 us (95%)
  between operations  14.3 us (2%)
  matrix products  8.12 us (1%)
    unnamed x8, waiting for transfers between devices  260 us
    psum x1, waiting for transfers between devices, spread(): return lax.psum(kept, axis)  132 us
    all_gather x1, waiting for transfers between devices, per_device(): gathered_two = lax.all_gather(panel_two, 'col', axis=0, tiled=True)  102 us
    all_gather x1, waiting for transfers between devices, per_device(): gathered_one = lax.all_gather(panel_one, 'col', axis=0, tiled=True)  92.3 us
    reduce_scatter x1, waiting for transfers between devices, per_device(): lax.psum_scatter((direct + parent_full).astype(jnp.bfloat16), 'row', scat...  69.3 us
  transfers between devices with their start and end apart: 6, of which 6 were waited for; matrix products, arithmetic and copies ran while one was open for 2% of the time, Pallas kernels for 0%

commit v1 on v0

v1 whole, which is shorter than its diff:
```python
import functools

import jax
import jax.numpy as jnp
from jax import lax
from jax.experimental import pallas as pl
from jax.experimental.pallas import tpu as pltpu
from jax.sharding import Mesh, PartitionSpec as P

ROW = ("ylo", "xh", "xl", "core")
COL = ("z", "yhi")
GROUP = ("xl", "core")
F32 = jnp.float32
BF16 = jnp.bfloat16
VMEM_LIMIT = 40 * 1024 * 1024


def params():
    return pltpu.CompilerParams(vmem_limit_bytes=VMEM_LIMIT)


def pack_kernel(idx, x_ref, out_ref):
    for s in range(8):
        out_ref[s] = x_ref[idx[s], :, 0:128]
    for s in range(4):
        block = idx[8 + s]
        out_ref[8 + 2 * s] = x_ref[block, :, 128:256]
        out_ref[9 + 2 * s] = x_ref[block, :, 256:384]


def pack(idx, x):
    return pl.pallas_call(
        pack_kernel,
        out_shape=jax.ShapeDtypeStruct((16, 16, 128), BF16),
        grid_spec=pltpu.PrefetchScalarGridSpec(
            num_scalar_prefetch=1,
            grid=(1,),
            in_specs=[pl.BlockSpec((16, 16, 384), lambda i, idx: (0, 0, 0))],
            out_specs=pl.BlockSpec((16, 16, 128), lambda i, idx: (0, 0, 0)),
        ),
        compiler_params=params(),
        name="pack",
    )(idx, x)


def upper_kernel(idx, g_ref, *refs):
    blocks = refs[:8]
    out_ref, own_ref = refs[8:10]
    panel, acc = refs[10:]
    s = pl.program_id(0)

    @pl.when(s == 0)
    def _():
        z = idx[12]
        for d in range(8):
            place = pl.multiple_of(lax.rem(z + 8 - d, 8) * 64, 64)
            for slot in range(8):
                for y in range(4):
                    panel[slot, pl.ds(place + y * 16, 16), :] = blocks[d][y, slot]
        acc[...] = jnp.zeros_like(acc)
        half = pl.multiple_of(idx[13] * 256, 256)
        rows = panel[idx[14], pl.ds(half, 256), :]
        own_ref[...] = jnp.where(idx[15] > 0, rows, jnp.zeros_like(rows))

    acc[...] += jnp.dot(g_ref[0], panel[s], preferred_element_type=F32)

    @pl.when(s == 7)
    def _():
        out_ref[...] = (-acc[...]).astype(BF16)


def upper(idx, g_all, blocks):
    whole = pl.BlockSpec((4, 8, 16, 128), lambda s, idx: (0, 0, 0, 0))
    flat = pl.BlockSpec((256, 128), lambda s, idx: (0, 0))
    return pl.pallas_call(
        upper_kernel,
        out_shape=(
            jax.ShapeDtypeStruct((256, 128), BF16),
            jax.ShapeDtypeStruct((256, 128), BF16),
        ),
        grid_spec=pltpu.PrefetchScalarGridSpec(
            num_scalar_prefetch=1,
            grid=(8,),
            in_specs=[pl.BlockSpec((1, 256, 512), lambda s, idx: (idx[s], 0, 0))] + [whole] * 8,
            out_specs=(flat, flat),
            scratch_shapes=[pltpu.VMEM((8, 512, 128), BF16), pltpu.VMEM((256, 128), F32)],
        ),
        compiler_params=params(),
        cost_estimate=pl.CostEstimate(
            flops=2 * 256 * 4096 * 128, bytes_accessed=3 * 1024 * 1024, transcendentals=0
        ),
        name="upper",
    )(idx, g_all, *blocks)


def cross_kernel(idx, lm_ref, gone_ref, link_ref, part_ref, *t_refs):
    gone = gone_ref[...]
    for h in range(4):
        part = lax.dot_general(
            lm_ref[h], gone, (((0,), (0,)), ((), ())), preferred_element_type=F32
        )
        part_ref[pl.ds(h * 128, 128), :] = part.astype(BF16)
    member = idx[16]
    for m in range(4):
        start = pl.multiple_of(jnp.bitwise_xor(member, m) * 256, 256)
        link = link_ref[:, pl.ds(start, 256)]
        term = jnp.dot(gone, link, preferred_element_type=F32)
        t_refs[m][...] = term.T.astype(BF16)


def cross(idx, lm, gone, link):
    term = pl.BlockSpec((256, 256), lambda i, idx: (0, 0))
    return pl.pallas_call(
        cross_kernel,
        out_shape=(jax.ShapeDtypeStruct((512, 128), BF16),)
        + (jax.ShapeDtypeStruct((256, 256), BF16),) * 4,
        grid_spec=pltpu.PrefetchScalarGridSpec(
            num_scalar_prefetch=1,
            grid=(1,),
            in_specs=[
                pl.BlockSpec((4, 256, 128), lambda i, idx: (0, 0, 0)),
                pl.BlockSpec((256, 128), lambda i, idx: (0, 0)),
                pl.BlockSpec((128, 1024), lambda i, idx: (0, 0)),
            ],
            out_specs=(pl.BlockSpec((512, 128), lambda i, idx: (0, 0)),) + (term,) * 4,
        ),
        compiler_params=params(),
        name="cross",
    )(idx, lm, gone, link)


def lower_kernel(idx, g_ref, m_ref, t0, t1, t2, t3, out_ref, acc):
    s = pl.program_id(0)

    @pl.when(s == 0)
    def _():
        acc[...] = jnp.zeros_like(acc)

    g = g_ref[0]
    for h in range(2):
        cols = m_ref[:, :, h].reshape(512, 128)
        acc[h] += jnp.dot(g, cols, preferred_element_type=F32)

    @pl.when(s == 3)
    def _():
        for h in range(2):
            rows = pl.ds(h * 128, 128)
            total = acc[h].T
            for t in (t0, t1, t2, t3):
                total += t[rows, :].astype(F32)
            out_ref[rows, :] = (-total).astype(BF16)


def lower(idx, g_all, m_two, terms):
    flat = pl.BlockSpec((256, 256), lambda s, idx: (0, 0))
    return pl.pallas_call(
        lower_kernel,
        out_shape=jax.ShapeDtypeStruct((256, 256), BF16),
        grid_spec=pltpu.PrefetchScalarGridSpec(
            num_scalar_prefetch=1,
            grid=(4,),
            in_specs=[
                pl.BlockSpec((1, 256, 512), lambda s, idx: (idx[8 + s], 0, 0)),
                pl.BlockSpec((8, 4, 2, 16, 128), lambda s, idx: (0, 0, s, 0, 0)),
            ]
            + [flat] * 4,
            out_specs=flat,
            scratch_shapes=[pltpu.VMEM((2, 256, 128), F32)],
        ),
        compiler_params=params(),
        cost_estimate=pl.CostEstimate(
            flops=2 * 256 * 2048 * 256, bytes_accessed=2 * 1024 * 1024, transcendentals=0
        ),
        name="lower",
    )(idx, g_all, m_two, *terms)


def per_device(ginv_top, panel_one, panel_two, parent_link, dinv_one, struct_one, struct_two):
    r = lax.axis_index(ROW)
    c = lax.axis_index(COL)
    z = lax.axis_index("z")
    member = lax.axis_index(GROUP)
    list_one = lax.dynamic_index_in_dim(struct_one, r // 4, 0, keepdims=False)
    list_two = lax.dynamic_index_in_dim(struct_two, r // 2, 0, keepdims=False)
    own = list_one == c // 2
    idx = jnp.concatenate(
        [
            list_one,
            list_two,
            jnp.stack([z, c % 2, jnp.argmax(own), jnp.any(own), member]).astype(jnp.int32),
        ]
    )

    g_all = lax.all_gather(ginv_top, ROW, axis=0, tiled=False)

    slots = jnp.concatenate(
        [panel_one.reshape(16, 16, 128), panel_two.reshape(16, 16, 256)], axis=2
    ).transpose(1, 0, 2)
    mine = lax.all_to_all(slots, ROW, 0, 0)
    packed = pack(idx, mine)
    across = lax.all_gather(packed, "yhi", axis=0, tiled=False)
    up_block, down_block = across[:, :8], across[:, 8:]

    m_two = lax.all_gather(down_block, "z", axis=0, tiled=False)

    up = [(i, (i + 1) % 8) for i in range(8)]
    down = [(i, (i - 1) % 8) for i in range(8)]
    blocks = [up_block] + [None] * 7
    a = b = up_block
    for s in range(1, 5):
        a = lax.ppermute(a, "z", up)
        blocks[s] = a
        if s < 4:
            b = lax.ppermute(b, "z", down)
            blocks[8 - s] = b

    ginv_one, own_rows = upper(idx, g_all, blocks)
    lm = lax.all_gather(own_rows, GROUP, axis=0, tiled=False)
    part, t0, t1, t2, t3 = cross(idx, lm, ginv_one, parent_link)
    t1 = lax.ppermute(t1, GROUP, [(i, i ^ 1) for i in range(4)])
    t2 = lax.ppermute(t2, GROUP, [(i, i ^ 2) for i in range(4)])
    t3 = lax.ppermute(t3, GROUP, [(i, i ^ 3) for i in range(4)])

    parts = lax.all_to_all(part.reshape(32, 16, 128), COL, 0, 0)
    diag_sum = jnp.sum(parts.astype(F32), axis=0)
    diag_one = (dinv_one.astype(F32) - diag_sum).astype(BF16)

    ginv_two = lower(idx, g_all, m_two, (t0, t1, t2, t3))
    return (ginv_one, diag_one, ginv_two)


def solution(mesh):
    fine = Mesh(mesh.devices.reshape(2, 2, 2, 2, 8, 4), ROW + COL)
    return jax.shard_map(
        per_device,
        mesh=fine,
        in_specs=(
            P(COL, ROW),
            P(ROW + COL, None),
            P(ROW + COL, None),
            P(ROW, None),
            P(COL, ROW),
            P(),
            P(),
        ),
        out_specs=(P(COL, ROW), P(COL, ROW), P(ROW, COL)),
        check_vma=False,
    )
```

time: 691 us -> 129 us (0.19)
  waiting for transfers between devices: 656 us -> 14.4 us
  starting transfers between devices: 0.24 us -> 51.5 us
  blocking collectives: 0 us -> 25.7 us
  matrix products: 8.12 us -> 0 us
  Pallas kernels: 0 us -> 7.91 us
    unnamed x8 -> x2, waiting for transfers between devices: 260 us -> 0.7 us
    all_gather x2, waiting for transfers between devices: 195 us -> 0.02 us  [the longest x1 0.02 us: per_device(): m_two = lax.all_gather(down_block, 'z', axis=0, tiled=False)]
    psum x1 -> x0, waiting for transfers between devices: 132 us -> none  [spread(): return lax.psum(kept, axis)]
    reduce_scatter x1 -> x0, waiting for transfers between devices: 69.3 us -> none  [per_device(): lax.psum_scatter((direct + parent_full).astype(jnp.bfloat16), 'row', scat...]
    ppermute x0 -> x10, starting transfers between devices: none -> 34.1 us  [the longest x3 18.1 us: per_device(): b = lax.ppermute(b, 'z', down)]
    all_gather x0 -> x2, blocking collectives: none -> 25.7 us  [the longest x1 13.6 us: per_device(): lm = lax.all_gather(own_rows, GROUP, axis=0, tiled=False)]
    all_to_all x0 -> x2, starting transfers between devices: none -> 17.3 us  [the longest x1 10.2 us: per_device(): mine = lax.all_to_all(slots, ROW, 0, 0)]
    ppermute x0 -> x10, waiting for transfers between devices: none -> 11.3 us  [the longest x4 6.67 us: per_device(): a = lax.ppermute(a, 'z', up)]
  transfers between devices with their start and end apart: 6 -> 14, of which waited for: 6 -> 7; matrix products, arithmetic and copies ran while one was open for 2% -> 5% of each run, Pallas kernels for 0% -> 6%
where the time goes in v1:
time: 129 us; the launch traced here: 128 us
  starting transfers between devices  51.5 us (40%)
  blocking collectives  25.7 us (20%)
  between operations  14.9 us (12%)
  waiting for transfers between devices  14.4 us (11%)
  local copies, waits for them, and re-layouts  9.68 us (8%)
  Pallas kernels  7.91 us (6%)
  other arithmetic  3.38 us (3%)
    ppermute x3, starting transfers between devices, per_device(): b = lax.ppermute(b, 'z', down)  18.1 us
    all_gather x1, blocking collectives, per_device(): lm = lax.all_gather(own_rows, GROUP, axis=0, tiled=False)  13.6 us
    all_gather x1, blocking collectives, per_device(): across = lax.all_gather(packed, 'yhi', axis=0, tiled=False)  12.2 us
    all_to_all x1, starting transfers between devices, per_device(): mine = lax.all_to_all(slots, ROW, 0, 0)  10.2 us
    ppermute x4, starting transfers between devices, per_device(): a = lax.ppermute(a, 'z', up)  8.2 us
    all_to_all x1, starting transfers between devices, per_device(): parts = lax.all_to_all(part.reshape(32, 16, 128), COL, 0, 0)  7.12 us
    ppermute x4, waiting for transfers between devices, per_device(): a = lax.ppermute(a, 'z', up)  6.67 us
    unnamed x14, local copies, waits for them, and re-layouts  6.46 us
  transfers between devices with their start and end apart: 14, of which 7 were waited for; matrix products, arithmetic and copies ran while one was open for 5% of the time, Pallas kernels for 6%

profile of v1, /device:TPU:1, one launch (start us, length us, event | category | flops | bytes accessed | tf_op | source)
XLA Modules:
  0.0 127.6 jit_solution(18051114375351524495)
XLA Ops:
  7.2 0.7 all-gather.7.cloned.1.call-update
  7.9 0.9 copy.18
  8.9 0.7 maximum_bitcast_fusion
  9.6 10.2 %all-to-all-start = ((bf16[16,16,384]{2,1,0:T(8,128)(2,1)}), bf16[16,16,384]{2,1,0:T(8,128)(2,1)S(1)}, u32[]{:S(2)}, u32[]{:S(2)}) async-start(bf16[16,16,384]{2,1,0:T(8,128)(2,1)} %maximum_bitcast_fusion), calls=%async_computation | async-start | bytes 393216 | tf_op jit(solution)/shard_map/all_to_all | solution.py:199
  19.9 1.3 %compare_reduce_fusion = (pred[]{:T(512)}, s32[8]{0:T(128)S(1)}) fusion(s32[]{:T(128)S(6)} %select_n.34, s32[4,8]{1,0:T(4,128)} %param.12, s32[]{:T(128)S(6)} %select_n.30), kind=kLoop, calls=%fused_computation.6 | loop fusion | flops 15 | bytes 73 | tf_op jit(solution)/shard_map/reduce_or | solution.py:190
  21.8 0.9 dynamic-slice_reduce_fusion
  22.7 0.7 compare_reduce_fusion.1
  23.4 0.8 concatenate.6.idx
  24.2 2.3 %all-to-all-done.x_ref = bf16[16,16,384]{2,1,0:T(8,128)(2,1)S(1)} async-done(((bf16[16,16,384]{2,1,0:T(8,128)(2,1)}), bf16[16,16,384]{2,1,0:T(8,128)(2,1)S(1)}, u32[]{:S(2)}, u32[]{:S(2)}) %all-to-all-start) | async-done | bytes 196640 | tf_op jit(solution)/shard_map/all_to_all | solution.py:199
  27.1 12.2 %all-gather.1 = bf16[64,16,128]{2,1,0:T(8,128)(2,1)S(1)} all-gather(bf16[16,16,128]{2,1,0:T(8,128)(2,1)S(1)} %pack.1), channel_id=3, replica_groups=mesh['ylo'=2,'xh'=2,'xl'=2,'core'=2,'z'=8,'yhi'=4] {'yhi'}, dimensions={0}, use_global_device_ids=true | all-gather | bytes 327680 | tf_op jit(solution)/shard_map/all_gather | solution.py:201
  39.9 2.5 %collective-permute-start = (bf16[4,8,16,128]{3,2,1,0:T(8,128)(2,1)S(1)}, bf16[4,8,16,128]{3,2,1,0:T(8,128)(2,1)S(1)}, u32[]{:S(2)}, u32[]{:S(2)}) collective-permute-start(bf16[4,8,16,128]{3,2,1,0:T(8,128)(2,1)S(1)} %get-tuple-element.22.refs_0_), channel_id=1, source_target_pairs={{0,4},{4,8},{8,12},{12,16},{16,20},{20,24},{24,28},{28,0},{1,5},{5... | collective-permute-start | bytes 393224 | tf_op jit(solution)/shard_map/ppermute | solution.py:211
  42.4 8.9 %collective-permute-start.4 = (bf16[4,8,16,128]{3,2,1,0:T(8,128)(2,1)S(1)}, bf16[4,8,16,128]{3,2,1,0:T(8,128)(2,1)S(1)}, u32[]{:S(2)}, u32[]{:S(2)}) collective-permute-start(bf16[4,8,16,128]{3,2,1,0:T(8,128)(2,1)S(1)} %get-tuple-element.22.refs_0_), channel_id=1, source_target_pairs={{0,28},{4,0},{8,4},{12,8},{16,12},{20,16},{24,20},{28,24},{1,29},{... | collective-permute-start | bytes 393224 | tf_op jit(solution)/shard_map/ppermute | solution.py:214
  51.8 1.9 %collective-permute-start.1 = (bf16[4,8,16,128]{3,2,1,0:T(8,128)(2,1)S(1)}, bf16[4,8,16,128]{3,2,1,0:T(8,128)(2,1)S(1)}, u32[]{:S(2)}, u32[]{:S(2)}) collective-permute-start(bf16[4,8,16,128]{3,2,1,0:T(8,128)(2,1)S(1)} %collective-permute-done.refs_1_), channel_id=1, source_target_pairs={{0,4},{4,8},{8,12},{12,16},{16,20},{20,24},{24,28},{28,0},{1,5},{5... | collective-permute-start | bytes 393224 | tf_op jit(solution)/shard_map/ppermute | solution.py:211
  53.7 4.6 %collective-permute-start.5 = (bf16[4,8,16,128]{3,2,1,0:T(8,128)(2,1)S(1)}, bf16[4,8,16,128]{3,2,1,0:T(8,128)(2,1)S(1)}, u32[]{:S(2)}, u32[]{:S(2)}) collective-permute-start(bf16[4,8,16,128]{3,2,1,0:T(8,128)(2,1)S(1)} %collective-permute-done.4.refs_7_), channel_id=1, source_target_pairs={{0,28},{4,0},{8,4},{12,8},{16,12},{20,16},{24,20},{28,24},{1,29},{... | collective-permute-start | bytes 393224 | tf_op jit(solution)/shard_map/ppermute | solution.py:214
  58.7 1.9 %collective-permute-start.2 = (bf16[4,8,16,128]{3,2,1,0:T(8,128)(2,1)S(1)}, bf16[4,8,16,128]{3,2,1,0:T(8,128)(2,1)S(1)}, u32[]{:S(2)}, u32[]{:S(2)}) collective-permute-start(bf16[4,8,16,128]{3,2,1,0:T(8,128)(2,1)S(1)} %collective-permute-done.1.refs_2_), channel_id=1, source_target_pairs={{0,4},{4,8},{8,12},{12,16},{16,20},{20,24},{24,28},{28,0},{1,5},{5... | collective-permute-start | bytes 393224 | tf_op jit(solution)/shard_map/ppermute | solution.py:211
  60.6 4.6 %collective-permute-start.6 = (bf16[4,8,16,128]{3,2,1,0:T(8,128)(2,1)S(1)}, bf16[4,8,16,128]{3,2,1,0:T(8,128)(2,1)S(1)}, u32[]{:S(2)}, u32[]{:S(2)}) collective-permute-start(bf16[4,8,16,128]{3,2,1,0:T(8,128)(2,1)S(1)} %collective-permute-done.5.refs_6_), channel_id=1, source_target_pairs={{0,28},{4,0},{8,4},{12,8},{16,12},{20,16},{24,20},{28,24},{1,29},{... | collective-permute-start | bytes 393224 | tf_op jit(solution)/shard_map/ppermute | solution.py:214
  65.6 1.9 %collective-permute-start.3 = (bf16[4,8,16,128]{3,2,1,0:T(8,128)(2,1)S(1)}, bf16[4,8,16,128]{3,2,1,0:T(8,128)(2,1)S(1)}, u32[]{:S(2)}, u32[]{:S(2)}) collective-permute-start(bf16[4,8,16,128]{3,2,1,0:T(8,128)(2,1)S(1)} %collective-permute-done.2.refs_3_), channel_id=1, source_target_pairs={{0,4},{4,8},{8,12},{12,16},{16,20},{20,24},{24,28},{28,0},{1,5},{5... | collective-permute-start | bytes 393224 | tf_op jit(solution)/shard_map/ppermute | solution.py:211
  67.5 5.5 %collective-permute-done.3.refs_4_ = bf16[4,8,16,128]{3,2,1,0:T(8,128)(2,1)S(1)} collective-permute-done((bf16[4,8,16,128]{3,2,1,0:T(8,128)(2,1)S(1)}, bf16[4,8,16,128]{3,2,1,0:T(8,128)(2,1)S(1)}, u32[]{:S(2)}, u32[]{:S(2)}) %collective-permute-start.3) | collective-permute-done | bytes 131104 | tf_op jit(solution)/shard_map/ppermute | solution.py:211
  73.0 2.2 %copy-done.1 = bf16[4096,512]{1,0:T(8,128)(2,1)S(1)} copy-done((bf16[4096,512]{1,0:T(8,128)(2,1)S(1)}, bf16[4096,512]{1,0:T(8,128)(2,1)}, u32[]{:S(2)}) %copy-start.1) | copy-done | bytes 4194328
  75.2 3.2 %upper.1 = (bf16[256,128]{1,0:T(8,128)(2,1)}, bf16[256,128]{1,0:T(8,128)(2,1)S(1)}) custom-call(s32[17]{0:T(128)S(1)} %concatenate.6.idx, bf16[16,256,512]{2,1,0:T(8,128)(2,1)S(1)} %bitcast.24, bf16[4,8,16,128]{3,2,1,0:T(8,128)(2,1)S(1)} %get-tuple-element.22.refs_0_, bf16[4,8,16,128]{3,2,1,0:T(8,128)(2,1)S(1)} %collective-permute-done.refs_1_, ...), custom_call_target="tpu_custom_call" | custom-call | flops 268435456 | bytes 3145728 | tf_op jit(solution)/shard_map/upper/pallas_call | solution.py:75
  78.4 13.6 %all-gather.2 = bf16[1024,128]{1,0:T(8,128)(2,1)S(1)} all-gather(bf16[256,128]{1,0:T(8,128)(2,1)S(1)} %get-tuple-element.13), channel_id=4, replica_groups=mesh['ylo'=2,'xh'=2,'xl'=2,'core'=2,'z'=8,'yhi'=4] {'xl','core'}, dimensions={0}, use_global_device_ids=true | all-gather | bytes 327680 | tf_op jit(solution)/shard_map/all_gather | solution.py:218
  92.0 0.8 copy-done.5
  92.8 1.5 %cross.1 = (bf16[512,128]{1,0:T(8,128)(2,1)}, bf16[256,256]{1,0:T(8,128)(2,1)S(1)}, bf16[256,256]{1,0:T(8,128)(2,1)S(1)}, bf16[256,256]{1,0:T(8,128)(2,1)S(1)}, bf16[256,256]{1,0:T(8,128)(2,1)S(1)}) custom-call(s32[17]{0:T(128)S(1)} %concatenate.6.idx, bf16[4,256,128]{2,1,0:T(8,128)(2,1)S(1)} %bitcast.26, bf16[256,128]{1,0:T(8,128)(2,1)S(1)} %copy-done.5, ...), custom_call_target="tpu_custom_call" | custom-call | tf_op jit(solution)/shard_map/cross/pallas_call | solution.py:113
  94.3 7.1 %all-to-all-start.1 = ((bf16[32,16,128]{2,1,0:T(8,128)(2,1)}), bf16[32,16,128]{2,1,0:T(8,128)(2,1)S(1)}, u32[]{:S(2)}, u32[]{:S(2)}) async-start(bf16[32,16,128]{2,1,0:T(8,128)(2,1)} %bitcast.10), calls=%async_computation.1 | async-start | bytes 262144 | tf_op jit(solution)/shard_map/all_to_all | solution.py:224
  101.4 2.3 %collective-permute-start.7 = (bf16[256,256]{1,0:T(8,128)(2,1)S(1)}, bf16[256,256]{1,0:T(8,128)(2,1)S(1)}, u32[]{:S(2)}, u32[]{:S(2)}) collective-permute-start(bf16[256,256]{1,0:T(8,128)(2,1)S(1)} %get-tuple-element.16), channel_id=1, source_target_pairs={{0,32},{32,0},{64,96},{96,64},{1,33},{33,1},{65,97},{97,65},{2,34}... | collective-permute-start | bytes 393224 | tf_op jit(solution)/shard_map/ppermute | solution.py:220
  103.7 2.1 %collective-permute-start.8 = (bf16[256,256]{1,0:T(8,128)(2,1)S(1)}, bf16[256,256]{1,0:T(8,128)(2,1)S(1)}, u32[]{:S(2)}, u32[]{:S(2)}) collective-permute-start(bf16[256,256]{1,0:T(8,128)(2,1)S(1)} %get-tuple-element.17), channel_id=1, source_target_pairs={{0,64},{32,96},{64,0},{96,32},{1,65},{33,97},{65,1},{97,33},{2,66}... | collective-permute-start | bytes 393224 | tf_op jit(solution)/shard_map/ppermute | solution.py:221
  105.9 3.4 %collective-permute-start.9 = (bf16[256,256]{1,0:T(8,128)(2,1)S(1)}, bf16[256,256]{1,0:T(8,128)(2,1)S(1)}, u32[]{:S(2)}, u32[]{:S(2)}) collective-permute-start(bf16[256,256]{1,0:T(8,128)(2,1)S(1)} %get-tuple-element.18), channel_id=1, source_target_pairs={{0,96},{32,64},{64,32},{96,0},{1,97},{33,65},{65,33},{97,1},{2,98}... | collective-permute-start | bytes 393224 | tf_op jit(solution)/shard_map/ppermute | solution.py:222
  109.3 1.4 %collective-permute-done.8.t2 = bf16[256,256]{1,0:T(8,128)(2,1)S(1)} collective-permute-done((bf16[256,256]{1,0:T(8,128)(2,1)S(1)}, bf16[256,256]{1,0:T(8,128)(2,1)S(1)}, u32[]{:S(2)}, u32[]{:S(2)}) %collective-permute-start.8) | collective-permute-done | bytes 131104 | tf_op jit(solution)/shard_map/ppermute | solution.py:221
  110.7 3.3 %collective-permute-done.9.t3 = bf16[256,256]{1,0:T(8,128)(2,1)S(1)} collective-permute-done((bf16[256,256]{1,0:T(8,128)(2,1)S(1)}, bf16[256,256]{1,0:T(8,128)(2,1)S(1)}, u32[]{:S(2)}, u32[]{:S(2)}) %collective-permute-start.9) | collective-permute-done | bytes 131104 | tf_op jit(solution)/shard_map/ppermute | solution.py:222
  114.0 2.2 %copy-done.2 = bf16[4096,512]{1,0:T(8,128)(2,1)S(1)} copy-done((bf16[4096,512]{1,0:T(8,128)(2,1)S(1)}, bf16[4096,512]{1,0:T(8,128)(2,1)}, u32[]{:S(2)}) %copy-start.2) | copy-done | bytes 4194328
  116.2 1.2 copy-done.3
  117.4 2.7 %lower.1 = bf16[256,256]{1,0:T(8,128)(2,1)} custom-call(s32[17]{0:T(128)S(1)} %concatenate.6.idx, bf16[16,256,512]{2,1,0:T(8,128)(2,1)S(1)} %bitcast.25, bf16[8,4,8,16,128]{4,3,2,1,0:T(8,128)(2,1)S(1)} %bitcast.27, bf16[256,256]{1,0:T(8,128)(2,1)S(1)} %get-tuple-element.15.t0, bf16[256,256]{1,0:T(8,128)(2,1)S(1)} %collective-permute-done.7.t1, ...), custom_call_target="tpu_custom_call" | custom-call | flops 268435456 | bytes 2097152 | tf_op jit(solution)/shard_map/lower/pallas_call | solution.py:156
  (28 shorter events, 3.2 us)
Async XLA Ops:
  7.2 1.7 %copy-start = (bf16[16,2048]{1,0:T(8,128)(2,1)S(1)}, bf16[16,2048]{1,0:T(8,128)(2,1)}, u32[]{:S(2)}) copy-start(bf16[16,2048]{1,0:T(8,128)(2,1)} %param.8) | copy-start | bytes 196612
  7.2 84.8 %copy-start.4 = (bf16[128,1024]{1,0:T(8,128)(2,1)S(1)}, bf16[128,1024]{1,0:T(8,128)(2,1)}, u32[]{:S(2)}) copy-start(bf16[128,1024]{1,0:T(8,128)(2,1)} %link_ref.1) | copy-start | bytes 786436
  7.2 65.8 %all-gather.7.cloned.1.call-start = ((), (), s32[]{:S(2)}) async-start(), calls=%async_computation.2 | async-start | bytes 4456448 | tf_op jit(solution)/shard_map/all_gather | solution.py:194
  9.6 16.9 %all-to-all-start = ((bf16[16,16,384]{2,1,0:T(8,128)(2,1)}), bf16[16,16,384]{2,1,0:T(8,128)(2,1)S(1)}, u32[]{:S(2)}, u32[]{:S(2)}) async-start(bf16[16,16,384]{2,1,0:T(8,128)(2,1)} %maximum_bitcast_fusion), calls=%async_computation | async-start | bytes 393216 | tf_op jit(solution)/shard_map/all_to_all | solution.py:199
  19.8 89.5 %all-gather.9.cloned.1.call-start = ((), (), s32[]{:S(2)}) async-start(), calls=%async_computation.3 | async-start | bytes 1179648 | tf_op jit(solution)/shard_map/all_gather | solution.py:204
  39.9 11.8 %collective-permute-start = (bf16[4,8,16,128]{3,2,1,0:T(8,128)(2,1)S(1)}, bf16[4,8,16,128]{3,2,1,0:T(8,128)(2,1)S(1)}, u32[]{:S(2)}, u32[]{:S(2)}) collective-permute-start(bf16[4,8,16,128]{3,2,1,0:T(8,128)(2,1)S(1)} %get-tuple-element.22.refs_0_), channel_id=1, source_target_pairs={{0,4},{4,8},{8,12},{12,16},{16,20},{20,24},{24,28},{28,0},{1,5},{5... | collective-permute-start | bytes 393224 | tf_op jit(solution)/shard_map/ppermute | solution.py:211
  42.4 11.3 %collective-permute-start.4 = (bf16[4,8,16,128]{3,2,1,0:T(8,128)(2,1)S(1)}, bf16[4,8,16,128]{3,2,1,0:T(8,128)(2,1)S(1)}, u32[]{:S(2)}, u32[]{:S(2)}) collective-permute-start(bf16[4,8,16,128]{3,2,1,0:T(8,128)(2,1)S(1)} %get-tuple-element.22.refs_0_), channel_id=1, source_target_pairs={{0,28},{4,0},{8,4},{12,8},{16,12},{20,16},{24,20},{28,24},{1,29},{... | collective-permute-start | bytes 393224 | tf_op jit(solution)/shard_map/ppermute | solution.py:214
  51.8 6.9 %collective-permute-start.1 = (bf16[4,8,16,128]{3,2,1,0:T(8,128)(2,1)S(1)}, bf16[4,8,16,128]{3,2,1,0:T(8,128)(2,1)S(1)}, u32[]{:S(2)}, u32[]{:S(2)}) collective-permute-start(bf16[4,8,16,128]{3,2,1,0:T(8,128)(2,1)S(1)} %collective-permute-done.refs_1_), channel_id=1, source_target_pairs={{0,4},{4,8},{8,12},{12,16},{16,20},{20,24},{24,28},{28,0},{1,5},{5... | collective-permute-start | bytes 393224 | tf_op jit(solution)/shard_map/ppermute | solution.py:211
  53.7 6.9 %collective-permute-start.5 = (bf16[4,8,16,128]{3,2,1,0:T(8,128)(2,1)S(1)}, bf16[4,8,16,128]{3,2,1,0:T(8,128)(2,1)S(1)}, u32[]{:S(2)}, u32[]{:S(2)}) collective-permute-start(bf16[4,8,16,128]{3,2,1,0:T(8,128)(2,1)S(1)} %collective-permute-done.4.refs_7_), channel_id=1, source_target_pairs={{0,28},{4,0},{8,4},{12,8},{16,12},{20,16},{24,20},{28,24},{1,29},{... | collective-permute-start | bytes 393224 | tf_op jit(solution)/shard_map/ppermute | solution.py:214
  58.7 6.9 %collective-permute-start.2 = (bf16[4,8,16,128]{3,2,1,0:T(8,128)(2,1)S(1)}, bf16[4,8,16,128]{3,2,1,0:T(8,128)(2,1)S(1)}, u32[]{:S(2)}, u32[]{:S(2)}) collective-permute-start(bf16[4,8,16,128]{3,2,1,0:T(8,128)(2,1)S(1)} %collective-permute-done.1.refs_2_), channel_id=1, source_target_pairs={{0,4},{4,8},{8,12},{12,16},{16,20},{20,24},{24,28},{28,0},{1,5},{5... | collective-permute-start | bytes 393224 | tf_op jit(solution)/shard_map/ppermute | solution.py:211
  60.6 6.9 %collective-permute-start.6 = (bf16[4,8,16,128]{3,2,1,0:T(8,128)(2,1)S(1)}, bf16[4,8,16,128]{3,2,1,0:T(8,128)(2,1)S(1)}, u32[]{:S(2)}, u32[]{:S(2)}) collective-permute-start(bf16[4,8,16,128]{3,2,1,0:T(8,128)(2,1)S(1)} %collective-permute-done.5.refs_6_), channel_id=1, source_target_pairs={{0,28},{4,0},{8,4},{12,8},{16,12},{20,16},{24,20},{28,24},{1,29},{... | collective-permute-start | bytes 393224 | tf_op jit(solution)/shard_map/ppermute | solution.py:214
  65.6 7.4 %collective-permute-start.3 = (bf16[4,8,16,128]{3,2,1,0:T(8,128)(2,1)S(1)}, bf16[4,8,16,128]{3,2,1,0:T(8,128)(2,1)S(1)}, u32[]{:S(2)}, u32[]{:S(2)}) collective-permute-start(bf16[4,8,16,128]{3,2,1,0:T(8,128)(2,1)S(1)} %collective-permute-done.2.refs_3_), channel_id=1, source_target_pairs={{0,4},{4,8},{8,12},{12,16},{16,20},{20,24},{24,28},{28,0},{1,5},{5... | collective-permute-start | bytes 393224 | tf_op jit(solution)/shard_map/ppermute | solution.py:211
  73.0 2.2 %copy-start.1 = (bf16[4096,512]{1,0:T(8,128)(2,1)S(1)}, bf16[4096,512]{1,0:T(8,128)(2,1)}, u32[]{:S(2)}) copy-start(bf16[4096,512]{1,0:T(8,128)(2,1)} %all-gather.7.cloned.1.call-done) | copy-start | bytes 12582916
  78.4 41.7 %copy-start.6 = (bf16[16,128]{1,0:T(8,128)(2,1)S(1)}, bf16[16,128]{1,0:T(8,128)(2,1)}, u32[]{:S(2)}) copy-start(bf16[16,128]{1,0:T(8,128)(2,1)} %param.11) | copy-start | bytes 12292
  91.9 0.8 copy-start.5
  94.3 25.8 %all-to-all-start.1 = ((bf16[32,16,128]{2,1,0:T(8,128)(2,1)}), bf16[32,16,128]{2,1,0:T(8,128)(2,1)S(1)}, u32[]{:S(2)}, u32[]{:S(2)}) async-start(bf16[32,16,128]{2,1,0:T(8,128)(2,1)} %bitcast.10), calls=%async_computation.1 | async-start | bytes 262144 | tf_op jit(solution)/shard_map/all_to_all | solution.py:224
  101.4 7.9 %collective-permute-start.7 = (bf16[256,256]{1,0:T(8,128)(2,1)S(1)}, bf16[256,256]{1,0:T(8,128)(2,1)S(1)}, u32[]{:S(2)}, u32[]{:S(2)}) collective-permute-start(bf16[256,256]{1,0:T(8,128)(2,1)S(1)} %get-tuple-element.16), channel_id=1, source_target_pairs={{0,32},{32,0},{64,96},{96,64},{1,33},{33,1},{65,97},{97,65},{2,34}... | collective-permute-start | bytes 393224 | tf_op jit(solution)/shard_map/ppermute | solution.py:220
  103.7 6.9 %collective-permute-start.8 = (bf16[256,256]{1,0:T(8,128)(2,1)S(1)}, bf16[256,256]{1,0:T(8,128)(2,1)S(1)}, u32[]{:S(2)}, u32[]{:S(2)}) collective-permute-start(bf16[256,256]{1,0:T(8,128)(2,1)S(1)} %get-tuple-element.17), channel_id=1, source_target_pairs={{0,64},{32,96},{64,0},{96,32},{1,65},{33,97},{65,1},{97,33},{2,66}... | collective-permute-start | bytes 393224 | tf_op jit(solution)/shard_map/ppermute | solution.py:221
  105.9 8.1 %collective-permute-start.9 = (bf16[256,256]{1,0:T(8,128)(2,1)S(1)}, bf16[256,256]{1,0:T(8,128)(2,1)S(1)}, u32[]{:S(2)}, u32[]{:S(2)}) collective-permute-start(bf16[256,256]{1,0:T(8,128)(2,1)S(1)} %get-tuple-element.18), channel_id=1, source_target_pairs={{0,96},{32,64},{64,32},{96,0},{1,97},{33,65},{65,33},{97,1},{2,98}... | collective-permute-start | bytes 393224 | tf_op jit(solution)/shard_map/ppermute | solution.py:222
  114.0 2.2 %copy-start.2 = (bf16[4096,512]{1,0:T(8,128)(2,1)S(1)}, bf16[4096,512]{1,0:T(8,128)(2,1)}, u32[]{:S(2)}) copy-start(bf16[4096,512]{1,0:T(8,128)(2,1)} %all-gather.7.cloned.1.call-done) | copy-start | bytes 12582916
  116.2 1.2 copy-start.3
Sparse Core Ops, SparseCore 0:
  10.2 50.3 all-gather.6
  63.2 37.3 all-gather.8

commit v2 on v1

v2 whole, which is shorter than its diff:
```python
import functools

import jax
import jax.numpy as jnp
from jax import lax
from jax.experimental import pallas as pl
from jax.experimental.pallas import tpu as pltpu
from jax.sharding import Mesh, PartitionSpec as P

ROW = ("ylo", "xh", "xl", "core")
COL = ("z", "yhi")
GROUP = ("xl", "core")
F32 = jnp.float32
BF16 = jnp.bfloat16
VMEM_LIMIT = 40 * 1024 * 1024


def params():
    return pltpu.CompilerParams(vmem_limit_bytes=VMEM_LIMIT)


def pack_kernel(idx, x_ref, out_ref):
    for s in range(8):
        out_ref[s] = x_ref[idx[s], :, 0:128]
    for s in range(4):
        block = idx[8 + s]
        out_ref[8 + 2 * s] = x_ref[block, :, 128:256]
        out_ref[9 + 2 * s] = x_ref[block, :, 256:384]


def pack(idx, x):
    return pl.pallas_call(
        pack_kernel,
        out_shape=jax.ShapeDtypeStruct((16, 16, 128), BF16),
        grid_spec=pltpu.PrefetchScalarGridSpec(
            num_scalar_prefetch=1,
            grid=(1,),
            in_specs=[pl.BlockSpec((16, 16, 384), lambda i, idx: (0, 0, 0))],
            out_specs=pl.BlockSpec((16, 16, 128), lambda i, idx: (0, 0, 0)),
        ),
        compiler_params=params(),
        name="pack",
    )(idx, x)


def upper_kernel(idx, g_ref, m_ref, near_ref, out_ref, acc):
    s = pl.program_id(0)

    @pl.when(s == 0)
    def _():
        acc[...] = jnp.zeros_like(acc)
        rows = near_ref[...].reshape(256, 128)
        out_ref[1] = jnp.where(idx[15] > 0, rows, jnp.zeros_like(rows))

    acc[...] += jnp.dot(g_ref[0], m_ref[...].reshape(512, 128), preferred_element_type=F32)

    @pl.when(s == 7)
    def _():
        out_ref[0] = (-acc[...]).astype(BF16)


def upper(idx, g_all, m_one):
    return pl.pallas_call(
        upper_kernel,
        out_shape=jax.ShapeDtypeStruct((2, 256, 128), BF16),
        grid_spec=pltpu.PrefetchScalarGridSpec(
            num_scalar_prefetch=1,
            grid=(8,),
            in_specs=[
                pl.BlockSpec((1, 256, 512), lambda s, idx: (idx[s], 0, 0)),
                pl.BlockSpec((8, 4, 1, 16, 128), lambda s, idx: (0, 0, s, 0, 0)),
                pl.BlockSpec((4, 4, 1, 16, 128), lambda s, idx: (idx[13], 0, idx[14], 0, 0)),
            ],
            out_specs=pl.BlockSpec((2, 256, 128), lambda s, idx: (0, 0, 0)),
            scratch_shapes=[pltpu.VMEM((256, 128), F32)],
        ),
        compiler_params=params(),
        cost_estimate=pl.CostEstimate(
            flops=2 * 256 * 4096 * 128, bytes_accessed=3 * 1024 * 1024, transcendentals=0
        ),
        name="upper",
    )(idx, g_all, m_one, m_one)


def cross_kernel(pair_ref, mine_ref, part_ref):
    gone = mine_ref[0]
    for h in range(4):
        part = lax.dot_general(
            pair_ref[h, 1], gone, (((0,), (0,)), ((), ())), preferred_element_type=F32
        )
        part_ref[pl.ds(h * 128, 128), :] = part.astype(BF16)


def cross(pairs, mine):
    return pl.pallas_call(
        cross_kernel,
        out_shape=jax.ShapeDtypeStruct((512, 128), BF16),
        compiler_params=params(),
        name="cross",
    )(pairs, mine)


def lower_kernel(idx, g_ref, m_ref, pair_ref, l0, l1, l2, l3, out_ref, acc):
    s = pl.program_id(0)

    @pl.when(s == 0)
    def _():
        member = idx[16]
        total = jnp.zeros((256, 256), F32)
        for m, link in enumerate((l0, l1, l2, l3)):
            gone = pair_ref[jnp.bitwise_xor(member, m), 0]
            total += jnp.dot(gone, link[...], preferred_element_type=F32)
        acc[0] = total[:, 0:128]
        acc[1] = total[:, 128:256]

    g = g_ref[0]
    for h in range(2):
        cols = m_ref[:, :, h].reshape(512, 128)
        acc[h] += jnp.dot(g, cols, preferred_element_type=F32)

    @pl.when(s == 3)
    def _():
        for h in range(2):
            out_ref[pl.ds(h * 128, 128), :] = (-acc[h].T).astype(BF16)


def lower(idx, g_all, m_two, pairs, links):
    flat = pl.BlockSpec((128, 256), lambda s, idx: (0, 0))
    return pl.pallas_call(
        lower_kernel,
        out_shape=jax.ShapeDtypeStruct((256, 256), BF16),
        grid_spec=pltpu.PrefetchScalarGridSpec(
            num_scalar_prefetch=1,
            grid=(4,),
            in_specs=[
                pl.BlockSpec((1, 256, 512), lambda s, idx: (idx[8 + s], 0, 0)),
                pl.BlockSpec((8, 4, 2, 16, 128), lambda s, idx: (0, 0, s, 0, 0)),
                pl.BlockSpec((4, 2, 256, 128), lambda s, idx: (0, 0, 0, 0)),
            ]
            + [flat] * 4,
            out_specs=pl.BlockSpec((256, 256), lambda s, idx: (0, 0)),
            scratch_shapes=[pltpu.VMEM((2, 256, 128), F32)],
        ),
        compiler_params=params(),
        cost_estimate=pl.CostEstimate(
            flops=2 * 256 * 2560 * 256, bytes_accessed=3 * 1024 * 1024, transcendentals=0
        ),
        name="lower",
    )(idx, g_all, m_two, pairs, *links)


def settle_kernel(dinv_ref, parts_ref, out_ref):
    total = jnp.sum(parts_ref[...].astype(F32), axis=0)
    out_ref[...] = (dinv_ref[...].astype(F32) - total).astype(BF16)


def settle(dinv, parts):
    return pl.pallas_call(
        settle_kernel,
        out_shape=jax.ShapeDtypeStruct((16, 128), BF16),
        compiler_params=params(),
        name="settle",
    )(dinv, parts)


def per_device(ginv_top, panel_one, panel_two, parent_link, dinv_one, struct_one, struct_two):
    r = lax.axis_index(ROW)
    c = lax.axis_index(COL)
    z = lax.axis_index("z")
    member = lax.axis_index(GROUP)
    list_one = lax.dynamic_index_in_dim(struct_one, r // 4, 0, keepdims=False)
    list_two = lax.dynamic_index_in_dim(struct_two, r // 2, 0, keepdims=False)
    own = list_one == c // 2
    idx = jnp.concatenate(
        [
            list_one,
            list_two,
            jnp.stack([z, c % 2, jnp.argmax(own), jnp.any(own), member]).astype(jnp.int32),
        ]
    )

    g_all = lax.all_gather(ginv_top, ROW, axis=0, tiled=False)

    slots = jnp.concatenate(
        [panel_one.reshape(16, 16, 128), panel_two.reshape(16, 16, 256)], axis=2
    ).transpose(1, 0, 2)
    mine = lax.all_to_all(slots, ROW, 0, 0)

    packed = pack(idx, mine)
    across = lax.all_gather(packed, "yhi", axis=0, tiled=False)
    up_block, down_block = across[:, :8], across[:, 8:]
    copies = jnp.broadcast_to(up_block, (8, 4, 8, 16, 128))

    copies, parent_link = lax.optimization_barrier((copies, parent_link))
    m_one = lax.all_to_all(copies, "z", 0, 0)
    links = []
    for m in range(4):
        to = jnp.bitwise_xor(member, m)
        link = lax.dynamic_slice_in_dim(parent_link, to * 256, 256, 1)
        if m:
            link = lax.ppermute(link, GROUP, [(i, i ^ m) for i in range(4)])
        links.append(link)
    g_all, down_block, *links = lax.optimization_barrier((g_all, down_block, *links))
    m_two = lax.all_gather(down_block, "z", axis=0, tiled=False)

    mine_one = upper(idx, g_all, m_one)
    pairs = lax.all_gather(mine_one, GROUP, axis=0, tiled=False)
    part = cross(pairs, mine_one)
    parts = lax.all_to_all(part.reshape(32, 16, 128), COL, 0, 0)
    diag_one = settle(dinv_one, parts)

    ginv_two = lower(idx, g_all, m_two, pairs, links)
    return (mine_one[0], diag_one, ginv_two)


def solution(mesh):
    fine = Mesh(mesh.devices.reshape(2, 2, 2, 2, 8, 4), ROW + COL)
    return jax.shard_map(
        per_device,
        mesh=fine,
        in_specs=(
            P(COL, ROW),
            P(ROW + COL, None),
            P(ROW + COL, None),
            P(ROW, None),
            P(COL, ROW),
            P(),
            P(),
        ),
        out_specs=(P(COL, ROW), P(COL, ROW), P(ROW, COL)),
        check_vma=False,
    )
```

time: 129 us -> 123 us (0.953)
  starting transfers between devices: 51.5 us -> 34.7 us
  waiting for transfers between devices: 14.4 us -> 29.1 us
  blocking collectives: 25.7 us -> 22.1 us
    ppermute x10 -> x3, starting transfers between devices: 34.1 us -> 10.6 us  [per_device(): link = lax.ppermute(link, GROUP, [(i, i ^ m) for i in range(4)])]
    all_to_all x0 -> x1, waiting for transfers between devices: none -> 14.1 us  [per_device(): m_one = lax.all_to_all(copies, 'z', 0, 0)]
    all_to_all x1, waiting for transfers between devices: 0.01 us -> 10.7 us  [per_device(): parts = lax.all_to_all(part.reshape(32, 16, 128), COL, 0, 0)]
    ppermute x10 -> x3, waiting for transfers between devices: 11.3 us -> 1.21 us  [per_device(): link = lax.ppermute(link, GROUP, [(i, i ^ m) for i in range(4)])]
    all_to_all x0 -> x1, starting transfers between devices: none -> 9.06 us  [per_device(): m_one = lax.all_to_all(copies, 'z', 0, 0)]
    all_gather x1, blocking collectives: 13.6 us -> 9.9 us  [per_device(): pairs = lax.all_gather(mine_one, GROUP, axis=0, tiled=False)]
    all_to_all x1, starting transfers between devices: 7.12 us -> 4.72 us  [per_device(): parts = lax.all_to_all(part.reshape(32, 16, 128), COL, 0, 0)]
    unnamed x14 -> x12, local copies, waits for them, and re-layouts: 6.46 us -> 5.66 us
  transfers between devices with their start and end apart: 14 -> 8, of which waited for: 7 -> 5; matrix products, arithmetic and copies ran while one was open for 5% -> 6% of each run, Pallas kernels for 6% -> 4%
where the time goes in v2:
time: 123 us; the launch traced here: 122 us
  starting transfers between devices  34.7 us (28%)
  waiting for transfers between devices  29.1 us (24%)
  blocking collectives  22.1 us (18%)
  between operations  14.8 us (12%)
  local copies, waits for them, and re-layouts  10.8 us (9%)
  Pallas kernels  7.68 us (6%)
  other arithmetic  2.74 us (2%)
    all_to_all x1, waiting for transfers between devices, per_device(): m_one = lax.all_to_all(copies, 'z', 0, 0)  14.1 us
    all_gather x1, blocking collectives, per_device(): across = lax.all_gather(packed, 'yhi', axis=0, tiled=False)  12.2 us
    all_to_all x1, waiting for transfers between devices, per_device(): parts = lax.all_to_all(part.reshape(32, 16, 128), COL, 0, 0)  10.7 us
    ppermute x3, starting transfers between devices, per_device(): link = lax.ppermute(link, GROUP, [(i, i ^ m) for i in range(4)])  10.6 us
    all_to_all x1, starting transfers between devices, per_device(): mine = lax.all_to_all(slots, ROW, 0, 0)  10.2 us
    all_gather x1, blocking collectives, per_device(): pairs = lax.all_gather(mine_one, GROUP, axis=0, tiled=False)  9.9 us
    all_to_all x1, starting transfers between devices, per_device(): m_one = lax.all_to_all(copies, 'z', 0, 0)  9.06 us
    unnamed x12, local copies, waits for them, and re-layouts  5.66 us
  transfers between devices with their start and end apart: 8, of which 5 were waited for; matrix products, arithmetic and copies ran while one was open for 6% of the time, Pallas kernels for 4%

profile of v2, /device:TPU:1, one launch (start us, length us, event | category | flops | bytes accessed | tf_op | source)
XLA Modules:
  0.0 121.9 jit_solution(1719440057529948497)
XLA Ops:
  7.2 0.0 all-gather.7.cloned.1.call-start
  7.2 0.7 all-gather.7.cloned.1.call-update
  7.9 0.9 copy.18
  8.9 0.7 maximum_bitcast_fusion
  9.6 10.2 %all-to-all-start = ((bf16[16,16,384]{2,1,0:T(8,128)(2,1)}), bf16[16,16,384]{2,1,0:T(8,128)(2,1)S(1)}, u32[]{:S(2)}, u32[]{:S(2)}) async-start(bf16[16,16,384]{2,1,0:T(8,128)(2,1)} %maximum_bitcast_fusion), calls=%async_computation | async-start | bytes 393216 | tf_op jit(solution)/shard_map/all_to_all | solution.py:187
  19.8 1.3 %compare_reduce_fusion = (pred[]{:T(512)}, s32[8]{0:T(128)S(1)}) fusion(s32[]{:T(128)S(6)} %select_n.46, s32[4,8]{1,0:T(4,128)} %param.12, s32[]{:T(128)S(6)} %select_n.42), kind=kLoop, calls=%fused_computation.10 | loop fusion | flops 15 | bytes 73 | tf_op jit(solution)/shard_map/reduce_or | solution.py:178
  21.7 0.9 dynamic-slice_reduce_fusion
  22.6 0.7 compare_reduce_fusion.1
  23.3 0.7 concatenate.6.idx
  24.0 2.5 %all-to-all-done.x_ref = bf16[16,16,384]{2,1,0:T(8,128)(2,1)S(1)} async-done(((bf16[16,16,384]{2,1,0:T(8,128)(2,1)}), bf16[16,16,384]{2,1,0:T(8,128)(2,1)S(1)}, u32[]{:S(2)}, u32[]{:S(2)}) %all-to-all-start) | async-done | bytes 196640 | tf_op jit(solution)/shard_map/all_to_all | solution.py:187
  26.5 0.6 pack.1
  27.1 12.2 %all-gather.1 = bf16[64,16,128]{2,1,0:T(8,128)(2,1)S(1)} all-gather(bf16[16,16,128]{2,1,0:T(8,128)(2,1)S(1)} %pack.1), channel_id=3, replica_groups=mesh['ylo'=2,'xh'=2,'xl'=2,'core'=2,'z'=8,'yhi'=4] {'yhi'}, dimensions={0}, use_global_device_ids=true | all-gather | bytes 327680 | tf_op jit(solution)/shard_map/all_gather | solution.py:190
  39.3 0.7 fusion.2
  39.9 1.2 %broadcast_in_dim.3 = bf16[8,4,8,16,128]{4,3,2,1,0:T(8,128)(2,1)} broadcast(bf16[4,8,16,128]{3,2,1,0:T(8,128)(2,1)S(1)} %get-tuple-element.27), dimensions={1,2,3,4} | broadcast | bytes 1179648 | tf_op jit(solution)/shard_map/broadcast_in_dim | solution.py:192
  41.2 9.1 %all-to-all-start.1 = ((bf16[8,4,8,16,128]{4,3,2,1,0:T(8,128)(2,1)}), bf16[8,4,8,16,128]{4,3,2,1,0:T(8,128)(2,1)S(1)}, u32[]{:S(2)}, u32[]{:S(2)}) async-start(bf16[8,4,8,16,128]{4,3,2,1,0:T(8,128)(2,1)} %broadcast_in_dim.3), calls=%async_computation.1 | async-start | bytes 2097152 | tf_op jit(solution)/shard_map/all_to_all | solution.py:195
  50.4 3.9 %collective-permute-start.2 = (bf16[128,256]{1,0:T(8,128)(2,1)S(1)}, bf16[128,256]{1,0:T(8,128)(2,1)S(1)}, u32[]{:S(2)}, u32[]{:S(2)}) collective-permute-start(bf16[128,256]{1,0:T(8,128)(2,1)S(1)} %get-tuple-element.23), channel_id=1, source_target_pairs={{0,96},{32,64},{64,32},{96,0},{1,97},{33,65},{65,33},{97,1},{2,98}... | collective-permute-start | bytes 196616 | tf_op jit(solution)/shard_map/ppermute | solution.py:201
  54.2 4.9 %collective-permute-start.1 = (bf16[128,256]{1,0:T(8,128)(2,1)S(1)}, bf16[128,256]{1,0:T(8,128)(2,1)S(1)}, u32[]{:S(2)}, u32[]{:S(2)}) collective-permute-start(bf16[128,256]{1,0:T(8,128)(2,1)S(1)} %get-tuple-element.24), channel_id=1, source_target_pairs={{0,64},{32,96},{64,0},{96,32},{1,65},{33,97},{65,1},{97,33},{2,66}... | collective-permute-start | bytes 196616 | tf_op jit(solution)/shard_map/ppermute | solution.py:201
  59.1 1.9 %collective-permute-start = (bf16[128,256]{1,0:T(8,128)(2,1)S(1)}, bf16[128,256]{1,0:T(8,128)(2,1)S(1)}, u32[]{:S(2)}, u32[]{:S(2)}) collective-permute-start(bf16[128,256]{1,0:T(8,128)(2,1)S(1)} %get-tuple-element.25), channel_id=1, source_target_pairs={{0,32},{32,0},{64,96},{96,64},{1,33},{33,1},{65,97},{97,65},{2,34}... | collective-permute-start | bytes 196616 | tf_op jit(solution)/shard_map/ppermute | solution.py:201
  61.0 0.2 collective-permute-done.1.l2
  61.2 1.0 collective-permute-done.l1
  62.3 14.1 %all-to-all-done.1.m_ref.near_ref = bf16[8,4,8,16,128]{4,3,2,1,0:T(8,128)(2,1)S(1)} async-done(((bf16[8,4,8,16,128]{4,3,2,1,0:T(8,128)(2,1)}), bf16[8,4,8,16,128]{4,3,2,1,0:T(8,128)(2,1)S(1)}, u32[]{:S(2)}, u32[]{:S(2)}) %all-to-all-start.1) | async-done | bytes 1048608 | tf_op jit(solution)/shard_map/all_to_all | solution.py:195
  76.4 2.2 %copy-done.1 = bf16[4096,512]{1,0:T(8,128)(2,1)S(1)} copy-done((bf16[4096,512]{1,0:T(8,128)(2,1)S(1)}, bf16[4096,512]{1,0:T(8,128)(2,1)}, u32[]{:S(2)}) %copy-start.1) | copy-done | bytes 4194328
  78.6 2.6 %upper.1.mine_ref = bf16[2,256,128]{2,1,0:T(8,128)(2,1)S(1)} custom-call(s32[17]{0:T(128)S(1)} %concatenate.6.idx, bf16[16,256,512]{2,1,0:T(8,128)(2,1)S(1)} %bitcast.26, bf16[8,4,8,16,128]{4,3,2,1,0:T(8,128)(2,1)S(1)} %all-to-all-done.1.m_ref.near_ref, bf16[8,4,8,16,128]{4,3,2,1,0:T(8,128)(2,1)S(1)} %all-to-all-done.1.m_ref.near_ref), custom_call_target="tpu_custom_call" | custom-call | flops 268435456 | bytes 3145728 | tf_op jit(solution)/shard_map/upper/pallas_call | solution.py:63
  81.2 9.9 %all-gather.2 = bf16[8,256,128]{2,1,0:T(8,128)(2,1)S(1)} all-gather(bf16[2,256,128]{2,1,0:T(8,128)(2,1)S(1)} %upper.1.mine_ref), channel_id=4, replica_groups=mesh['ylo'=2,'xh'=2,'xl'=2,'core'=2,'z'=8,'yhi'=4] {'xl','core'}, dimensions={0}, use_global_device_ids=true | all-gather | bytes 655360 | tf_op jit(solution)/shard_map/all_gather | solution.py:207
  91.2 0.9 cross.1
  92.1 4.7 %all-to-all-start.2 = ((bf16[32,16,128]{2,1,0:T(8,128)(2,1)}), bf16[32,16,128]{2,1,0:T(8,128)(2,1)S(1)}, u32[]{:S(2)}, u32[]{:S(2)}) async-start(bf16[32,16,128]{2,1,0:T(8,128)(2,1)} %bitcast.11), calls=%async_computation.2 | async-start | bytes 262144 | tf_op jit(solution)/shard_map/all_to_all | solution.py:209
  96.8 0.6 slice_bitcast_fusion
  97.4 10.7 %all-to-all-done.2.parts_ref = bf16[32,16,128]{2,1,0:T(8,128)(2,1)S(1)} async-done(((bf16[32,16,128]{2,1,0:T(8,128)(2,1)}), bf16[32,16,128]{2,1,0:T(8,128)(2,1)S(1)}, u32[]{:S(2)}, u32[]{:S(2)}) %all-to-all-start.2) | async-done | bytes 131104 | tf_op jit(solution)/shard_map/all_to_all | solution.py:209
  108.1 0.6 settle.1
  108.7 2.2 %copy-done.2 = bf16[4096,512]{1,0:T(8,128)(2,1)S(1)} copy-done((bf16[4096,512]{1,0:T(8,128)(2,1)S(1)}, bf16[4096,512]{1,0:T(8,128)(2,1)}, u32[]{:S(2)}) %copy-start.2) | copy-done | bytes 4194328
  110.9 1.2 %copy-done.3 = bf16[32,8,16,128]{3,2,1,0:T(8,128)(2,1)S(1)} copy-done((bf16[32,8,16,128]{3,2,1,0:T(8,128)(2,1)S(1)}, bf16[32,8,16,128]{3,2,1,0:T(8,128)(2,1)}, u32[]{:S(2)}) %copy-start.3) | copy-done | bytes 1048600
  112.2 2.9 %lower.1 = bf16[256,256]{1,0:T(8,128)(2,1)} custom-call(s32[17]{0:T(128)S(1)} %concatenate.6.idx, bf16[16,256,512]{2,1,0:T(8,128)(2,1)S(1)} %bitcast.27, bf16[8,4,8,16,128]{4,3,2,1,0:T(8,128)(2,1)S(1)} %bitcast.30, bf16[4,2,256,128]{3,2,1,0:T(8,128)(2,1)S(1)} %bitcast.29, bf16[128,256]{1,0:T(8,128)(2,1)S(1)} %get-tuple-element.17.l0, ...), custom_call_target="tpu_custom_call" | custom-call | flops 335544320 | bytes 3145728 | tf_op jit(solution)/shard_map/lower/pallas_call | solution.py:129
  (16 shorter events, 0.1 us)
Async XLA Ops:
  7.2 1.7 %copy-start = (bf16[16,2048]{1,0:T(8,128)(2,1)S(1)}, bf16[16,2048]{1,0:T(8,128)(2,1)}, u32[]{:S(2)}) copy-start(bf16[16,2048]{1,0:T(8,128)(2,1)} %param.8) | copy-start | bytes 196612
  7.2 43.1 %copy-start.5 = (bf16[128,1024]{1,0:T(8,128)(2,1)S(1)}, bf16[128,1024]{1,0:T(8,128)(2,1)}, u32[]{:S(2)}) copy-start(bf16[128,1024]{1,0:T(8,128)(2,1)} %param.10) | copy-start | bytes 786436
  7.2 55.1 %all-gather.7.cloned.1.call-start = ((), (), s32[]{:S(2)}) async-start(), calls=%async_computation.3 | async-start | bytes 4456448 | tf_op jit(solution)/shard_map/all_gather | solution.py:182
  9.6 16.9 %all-to-all-start = ((bf16[16,16,384]{2,1,0:T(8,128)(2,1)}), bf16[16,16,384]{2,1,0:T(8,128)(2,1)S(1)}, u32[]{:S(2)}, u32[]{:S(2)}) async-start(bf16[16,16,384]{2,1,0:T(8,128)(2,1)} %maximum_bitcast_fusion), calls=%async_computation | async-start | bytes 393216 | tf_op jit(solution)/shard_map/all_to_all | solution.py:187
  41.2 35.2 %all-to-all-start.1 = ((bf16[8,4,8,16,128]{4,3,2,1,0:T(8,128)(2,1)}), bf16[8,4,8,16,128]{4,3,2,1,0:T(8,128)(2,1)S(1)}, u32[]{:S(2)}, u32[]{:S(2)}) async-start(bf16[8,4,8,16,128]{4,3,2,1,0:T(8,128)(2,1)} %broadcast_in_dim.3), calls=%async_computation.1 | async-start | bytes 2097152 | tf_op jit(solution)/shard_map/all_to_all | solution.py:195
  50.2 58.5 %all-gather.9.cloned.1.call-start = ((), (), s32[]{:S(2)}) async-start(), calls=%async_computation.4 | async-start | bytes 1179648 | tf_op jit(solution)/shard_map/all_gather | solution.py:204
  50.4 10.7 %collective-permute-start.2 = (bf16[128,256]{1,0:T(8,128)(2,1)S(1)}, bf16[128,256]{1,0:T(8,128)(2,1)S(1)}, u32[]{:S(2)}, u32[]{:S(2)}) collective-permute-start(bf16[128,256]{1,0:T(8,128)(2,1)S(1)} %get-tuple-element.23), channel_id=1, source_target_pairs={{0,96},{32,64},{64,32},{96,0},{1,97},{33,65},{65,33},{97,1},{2,98}... | collective-permute-start | bytes 196616 | tf_op jit(solution)/shard_map/ppermute | solution.py:201
  54.2 7.0 %collective-permute-start.1 = (bf16[128,256]{1,0:T(8,128)(2,1)S(1)}, bf16[128,256]{1,0:T(8,128)(2,1)S(1)}, u32[]{:S(2)}, u32[]{:S(2)}) collective-permute-start(bf16[128,256]{1,0:T(8,128)(2,1)S(1)} %get-tuple-element.24), channel_id=1, source_target_pairs={{0,64},{32,96},{64,0},{96,32},{1,65},{33,97},{65,1},{97,33},{2,66}... | collective-permute-start | bytes 196616 | tf_op jit(solution)/shard_map/ppermute | solution.py:201
  59.1 3.1 %collective-permute-start = (bf16[128,256]{1,0:T(8,128)(2,1)S(1)}, bf16[128,256]{1,0:T(8,128)(2,1)S(1)}, u32[]{:S(2)}, u32[]{:S(2)}) collective-permute-start(bf16[128,256]{1,0:T(8,128)(2,1)S(1)} %get-tuple-element.25), channel_id=1, source_target_pairs={{0,32},{32,0},{64,96},{96,64},{1,33},{33,1},{65,97},{97,65},{2,34}... | collective-permute-start | bytes 196616 | tf_op jit(solution)/shard_map/ppermute | solution.py:201
  62.2 45.9 %copy-start.4 = (bf16[16,128]{1,0:T(8,128)(2,1)S(1)}, bf16[16,128]{1,0:T(8,128)(2,1)}, u32[]{:S(2)}) copy-start(bf16[16,128]{1,0:T(8,128)(2,1)} %dinv_ref.1) | copy-start | bytes 12292
  76.4 2.2 %copy-start.1 = (bf16[4096,512]{1,0:T(8,128)(2,1)S(1)}, bf16[4096,512]{1,0:T(8,128)(2,1)}, u32[]{:S(2)}) copy-start(bf16[4096,512]{1,0:T(8,128)(2,1)} %all-gather.7.cloned.1.call-done) | copy-start | bytes 12582916
  92.1 16.0 %all-to-all-start.2 = ((bf16[32,16,128]{2,1,0:T(8,128)(2,1)}), bf16[32,16,128]{2,1,0:T(8,128)(2,1)S(1)}, u32[]{:S(2)}, u32[]{:S(2)}) async-start(bf16[32,16,128]{2,1,0:T(8,128)(2,1)} %bitcast.11), calls=%async_computation.2 | async-start | bytes 262144 | tf_op jit(solution)/shard_map/all_to_all | solution.py:209
  108.7 2.2 %copy-start.2 = (bf16[4096,512]{1,0:T(8,128)(2,1)S(1)}, bf16[4096,512]{1,0:T(8,128)(2,1)}, u32[]{:S(2)}) copy-start(bf16[4096,512]{1,0:T(8,128)(2,1)} %all-gather.7.cloned.1.call-done) | copy-start | bytes 12582916
  110.9 1.2 %copy-start.3 = (bf16[32,8,16,128]{3,2,1,0:T(8,128)(2,1)S(1)}, bf16[32,8,16,128]{3,2,1,0:T(8,128)(2,1)}, u32[]{:S(2)}) copy-start(bf16[32,8,16,128]{3,2,1,0:T(8,128)(2,1)} %all-gather.9.cloned.1.call-done) | copy-start | bytes 3145732
Sparse Core Ops, SparseCore 0:
  10.2 50.5 all-gather.6
  63.4 38.2 all-gather.8

commit v3 on v2

--- a/solution.py
+++ b/solution.py
@@ -12,7 +12,7 @@
 GROUP = ("xl", "core")
 F32 = jnp.float32
 BF16 = jnp.bfloat16
-VMEM_LIMIT = 40 * 1024 * 1024
+VMEM_LIMIT = 24 * 1024 * 1024
 
 
 def params():
@@ -23,7 +23,7 @@
     for s in range(8):
         out_ref[s] = x_ref[idx[s], :, 0:128]
     for s in range(4):
-        block = idx[8 + s]
+        block = idx[17 + s]
         out_ref[8 + 2 * s] = x_ref[block, :, 128:256]
         out_ref[9 + 2 * s] = x_ref[block, :, 256:384]
 
@@ -43,43 +43,60 @@
     )(idx, x)
 
 
-def upper_kernel(idx, g_ref, m_ref, near_ref, out_ref, acc):
-    s = pl.program_id(0)
-
-    @pl.when(s == 0)
-    def _():
-        acc[...] = jnp.zeros_like(acc)
-        rows = near_ref[...].reshape(256, 128)
-        out_ref[1] = jnp.where(idx[15] > 0, rows, jnp.zeros_like(rows))
-
-    acc[...] += jnp.dot(g_ref[0], m_ref[...].reshape(512, 128), preferred_element_type=F32)
-
-    @pl.when(s == 7)
-    def _():
-        out_ref[0] = (-acc[...]).astype(BF16)
-
-
-def upper(idx, g_all, m_one):
+def choose_kernel(idx, g_ref, out_ref, sem):
+    copies = [pltpu.make_async_copy(g_ref.at[idx[s]], out_ref.at[s], sem.at[s]) for s in range(8)]
+    for copy in copies:
+        copy.start()
+    for copy in copies:
+        copy.wait()
+
+
+def choose(idx, g_all):
+    return pl.pallas_call(
+        choose_kernel,
+        out_shape=jax.ShapeDtypeStruct((8, 256, 512), BF16),
+        grid_spec=pltpu.PrefetchScalarGridSpec(
+            num_scalar_prefetch=1,
+            grid=(1,),
+            in_specs=[pl.BlockSpec(memory_space=pl.ANY)],
+            out_specs=pl.BlockSpec(memory_space=pl.ANY),
+            scratch_shapes=[pltpu.SemaphoreType.DMA((8,))],
+        ),
+        compiler_params=params(),
+        name="choose",
+    )(idx, g_all)
+
+
+def whole(shape):
+    return pl.BlockSpec(shape, lambda i, idx: (0,) * len(shape))
+
+
+def upper_kernel(idx, g_ref, m_ref, out_ref):
+    rows = m_ref[pl.ds(idx[13] * 4, 4), :, idx[14]].reshape(256, 128)
+    out_ref[1] = jnp.where(idx[15] > 0, rows, jnp.zeros_like(rows))
+    acc = jnp.zeros((256, 128), F32)
+    for s in range(8):
+        cols = m_ref[:, :, s].reshape(512, 128)
+        acc += jnp.dot(g_ref[s], cols, preferred_element_type=F32)
+    out_ref[0] = (-acc).astype(BF16)
+
+
+def upper(idx, g_own, m_one):
     return pl.pallas_call(
         upper_kernel,
         out_shape=jax.ShapeDtypeStruct((2, 256, 128), BF16),
         grid_spec=pltpu.PrefetchScalarGridSpec(
             num_scalar_prefetch=1,
-            grid=(8,),
-            in_specs=[
-                pl.BlockSpec((1, 256, 512), lambda s, idx: (idx[s], 0, 0)),
-                pl.BlockSpec((8, 4, 1, 16, 128), lambda s, idx: (0, 0, s, 0, 0)),
-                pl.BlockSpec((4, 4, 1, 16, 128), lambda s, idx: (idx[13], 0, idx[14], 0, 0)),
-            ],
-            out_specs=pl.BlockSpec((2, 256, 128), lambda s, idx: (0, 0, 0)),
-            scratch_shapes=[pltpu.VMEM((256, 128), F32)],
+            grid=(1,),
+            in_specs=[whole((8, 256, 512)), whole((8, 4, 8, 16, 128))],
+            out_specs=whole((2, 256, 128)),
         ),
         compiler_params=params(),
         cost_estimate=pl.CostEstimate(
             flops=2 * 256 * 4096 * 128, bytes_accessed=3 * 1024 * 1024, transcendentals=0
         ),
         name="upper",
-    )(idx, g_all, m_one, m_one)
+    )(idx, g_own, m_one)
 
 
 def cross_kernel(pair_ref, mine_ref, part_ref):
@@ -100,53 +117,61 @@
     )(pairs, mine)
 
 
-def lower_kernel(idx, g_ref, m_ref, pair_ref, l0, l1, l2, l3, out_ref, acc):
-    s = pl.program_id(0)
-
-    @pl.when(s == 0)
-    def _():
-        member = idx[16]
-        total = jnp.zeros((256, 256), F32)
+def through_kernel(idx, pair_ref, l0, l1, l2, l3, out_ref):
+    member = idx[16]
+    for h in range(2):
+        acc = jnp.zeros((256, 128), F32)
         for m, link in enumerate((l0, l1, l2, l3)):
             gone = pair_ref[jnp.bitwise_xor(member, m), 0]
-            total += jnp.dot(gone, link[...], preferred_element_type=F32)
-        acc[0] = total[:, 0:128]
-        acc[1] = total[:, 128:256]
-
-    g = g_ref[0]
+            cols = link[:, h * 128 : (h + 1) * 128]
+            acc += jnp.dot(gone, cols, preferred_element_type=F32)
+        out_ref[h] = acc
+
+
+def through(idx, pairs, links):
+    return pl.pallas_call(
+        through_kernel,
+        out_shape=jax.ShapeDtypeStruct((2, 256, 128), F32),
+        grid_spec=pltpu.PrefetchScalarGridSpec(
+            num_scalar_prefetch=1,
+            grid=(1,),
+            in_specs=[whole((4, 2, 256, 128))] + [whole((128, 256))] * 4,
+            out_specs=whole((2, 256, 128)),
+        ),
+        compiler_params=params(),
+        name="through",
+    )(idx, pairs, *links)
+
+
+def lower_kernel(idx, g_ref, m_ref, add_ref, out_ref):
     for h in range(2):
-        cols = m_ref[:, :, h].reshape(512, 128)
-        acc[h] += jnp.dot(g, cols, preferred_element_type=F32)
-
-    @pl.when(s == 3)
-    def _():
-        for h in range(2):
-            out_ref[pl.ds(h * 128, 128), :] = (-acc[h].T).astype(BF16)
-
-
-def lower(idx, g_all, m_two, pairs, links):
-    flat = pl.BlockSpec((128, 256), lambda s, idx: (0, 0))
+        acc = add_ref[h]
+        for s in range(4):
+            cols = m_ref[:, :, 2 * s + h].reshape(512, 128)
+            acc += jnp.dot(g_ref[idx[8 + s]], cols, preferred_element_type=F32)
+        out_ref[h * 128 : (h + 1) * 128, :] = (-acc.T).astype(BF16)
+
+
+def lower(idx, g_own, m_two, add):
     return pl.pallas_call(
         lower_kernel,
         out_shape=jax.ShapeDtypeStruct((256, 256), BF16),
         grid_spec=pltpu.PrefetchScalarGridSpec(
             num_scalar_prefetch=1,
-            grid=(4,),
+            grid=(1,),
             in_specs=[
-                pl.BlockSpec((1, 256, 512), lambda s, idx: (idx[8 + s], 0, 0)),
-                pl.BlockSpec((8, 4, 2, 16, 128), lambda s, idx: (0, 0, s, 0, 0)),
-                pl.BlockSpec((4, 2, 256, 128), lambda s, idx: (0, 0, 0, 0)),
-            ]
-            + [flat] * 4,
-            out_specs=pl.BlockSpec((256, 256), lambda s, idx: (0, 0)),
-            scratch_shapes=[pltpu.VMEM((2, 256, 128), F32)],
+                whole((8, 256, 512)),
+                whole((8, 4, 8, 16, 128)),
+                whole((2, 256, 128)),
+            ],
+            out_specs=whole((256, 256)),
         ),
         compiler_params=params(),
         cost_estimate=pl.CostEstimate(
-            flops=2 * 256 * 2560 * 256, bytes_accessed=3 * 1024 * 1024, transcendentals=0
+            flops=2 * 256 * 2048 * 256, bytes_accessed=3 * 1024 * 1024, transcendentals=0
         ),
         name="lower",
-    )(idx, g_all, m_two, pairs, *links)
+    )(idx, g_own, m_two, add)
 
 
 def settle_kernel(dinv_ref, parts_ref, out_ref):
@@ -171,12 +196,10 @@
     list_one = lax.dynamic_index_in_dim(struct_one, r // 4, 0, keepdims=False)
     list_two = lax.dynamic_index_in_dim(struct_two, r // 2, 0, keepdims=False)
     own = list_one == c // 2
+    place_two = jnp.argmax(list_one[None, :] == list_two[:, None], axis=1)
+    here = jnp.stack([z, c % 2, jnp.argmax(own), jnp.any(own), member])
     idx = jnp.concatenate(
-        [
-            list_one,
-            list_two,
-            jnp.stack([z, c % 2, jnp.argmax(own), jnp.any(own), member]).astype(jnp.int32),
-        ]
+        [list_one, place_two.astype(jnp.int32), here.astype(jnp.int32), list_two]
     )
 
     g_all = lax.all_gather(ginv_top, ROW, axis=0, tiled=False)
@@ -202,14 +225,16 @@
         links.append(link)
     g_all, down_block, *links = lax.optimization_barrier((g_all, down_block, *links))
     m_two = lax.all_gather(down_block, "z", axis=0, tiled=False)
-
-    mine_one = upper(idx, g_all, m_one)
+    g_own = choose(idx, g_all)
+    m_one, g_own = lax.optimization_barrier((m_one, g_own))
+
+    mine_one = upper(idx, g_own, m_one)
     pairs = lax.all_gather(mine_one, GROUP, axis=0, tiled=False)
     part = cross(pairs, mine_one)
     parts = lax.all_to_all(part.reshape(32, 16, 128), COL, 0, 0)
     diag_one = settle(dinv_one, parts)
 
-    ginv_two = lower(idx, g_all, m_two, pairs, links)
+    ginv_two = lower(idx, g_own, m_two, through(idx, pairs, links))
     return (mine_one[0], diag_one, ginv_two)
 
 

time: 123 us -> 117 us (0.951)
  waiting for transfers between devices: 29.1 us -> 23.7 us
  local copies, waits for them, and re-layouts: 10.8 us -> 9.45 us
    all_to_all x1, waiting for transfers between devices: 14.1 us -> 11.1 us  [per_device(): m_one = lax.all_to_all(copies, 'z', 0, 0)]
    all_to_all x1, waiting for transfers between devices: 10.7 us -> 9.01 us  [per_device(): parts = lax.all_to_all(part.reshape(32, 16, 128), COL, 0, 0)]
    pallas_call x0 -> x2, Pallas kernels: none -> 1.59 us  [the longest x1 0.81 us: through(): pl.pallas_call(through_kernel, out_shape=jax.ShapeDtypeStruct((2, 256, 12...]
    pallas_call x1, Pallas kernels: 2.64 us -> 1.24 us  [upper(): pl.pallas_call(upper_kernel, out_shape=jax.ShapeDtypeStruct((2, 256, 128)...]
    unnamed x12 -> x14, local copies, waits for them, and re-layouts: 5.66 us -> 4.28 us
  transfers between devices with their start and end apart: 8 -> 8, of which waited for: 5 -> 5; matrix products, arithmetic and copies ran while one was open for 6% -> 7% of each run, Pallas kernels for 4% -> 4%
where the time goes in v3:
time: 117 us; the launch traced here: 115 us
  starting transfers between devices  34.6 us (30%)
  waiting for transfers between devices  23.7 us (20%)
  blocking collectives  22.1 us (19%)
  between operations  14.9 us (13%)
  local copies, waits for them, and re-layouts  9.45 us (8%)
  Pallas kernels  6.91 us (6%)
  other arithmetic  3.45 us (3%)
    all_gather x1, blocking collectives, per_device(): across = lax.all_gather(packed, 'yhi', axis=0, tiled=False)  12.2 us
    all_to_all x1, waiting for transfers between devices, per_device(): m_one = lax.all_to_all(copies, 'z', 0, 0)  11.1 us
    ppermute x3, starting transfers between devices, per_device(): link = lax.ppermute(link, GROUP, [(i, i ^ m) for i in range(4)])  10.6 us
    all_to_all x1, starting transfers between devices, per_device(): mine = lax.all_to_all(slots, ROW, 0, 0)  10.2 us
    all_gather x1, blocking collectives, per_device(): pairs = lax.all_gather(mine_one, GROUP, axis=0, tiled=False)  9.94 us
    all_to_all x1, starting transfers between devices, per_device(): m_one = lax.all_to_all(copies, 'z', 0, 0)  9.06 us
    all_to_all x1, waiting for transfers between devices, per_device(): parts = lax.all_to_all(part.reshape(32, 16, 128), COL, 0, 0)  9.01 us
    all_to_all x1, starting transfers between devices, per_device(): parts = lax.all_to_all(part.reshape(32, 16, 128), COL, 0, 0)  4.67 us
  transfers between devices with their start and end apart: 8, of which 5 were waited for; matrix products, arithmetic and copies ran while one was open for 7% of the time, Pallas kernels for 4%

profile of v3, /device:TPU:1, one launch (start us, length us, event | category | flops | bytes accessed | tf_op | source)
XLA Modules:
  0.0 115.1 jit_solution(9044647167926624972)
XLA Ops:
  7.2 0.7 all-gather.7.cloned.1.call-update
  7.9 0.9 copy.20
  8.9 0.7 maximum_bitcast_fusion
  9.6 10.2 %all-to-all-start = ((bf16[16,16,384]{2,1,0:T(8,128)(2,1)}), bf16[16,16,384]{2,1,0:T(8,128)(2,1)S(1)}, u32[]{:S(2)}, u32[]{:S(2)}) async-start(bf16[16,16,384]{2,1,0:T(8,128)(2,1)} %maximum_bitcast_fusion), calls=%async_computation | async-start | bytes 393216 | tf_op jit(solution)/shard_map/all_to_all | solution.py:210
  19.8 1.3 %compare_reduce_fusion = (pred[]{:T(512)}, s32[8]{0:T(128)S(1)}) fusion(s32[]{:T(128)S(6)} %select_n.50, s32[4,8]{1,0:T(4,128)} %param.12, s32[]{:T(128)S(6)} %select_n.46), kind=kLoop, calls=%fused_computation.11 | loop fusion | flops 15 | bytes 73 | tf_op jit(solution)/shard_map/reduce_or | solution.py:200
  21.7 0.9 dynamic-slice_reduce_fusion
  22.6 0.7 compare_reduce_fusion.1
  23.3 0.7 iota_reduce_fusion
  24.0 0.8 concatenate.6.idx
  24.8 1.7 %all-to-all-done.x_ref = bf16[16,16,384]{2,1,0:T(8,128)(2,1)S(1)} async-done(((bf16[16,16,384]{2,1,0:T(8,128)(2,1)}), bf16[16,16,384]{2,1,0:T(8,128)(2,1)S(1)}, u32[]{:S(2)}, u32[]{:S(2)}) %all-to-all-start) | async-done | bytes 196640 | tf_op jit(solution)/shard_map/all_to_all | solution.py:210
  27.1 12.2 %all-gather = bf16[64,16,128]{2,1,0:T(8,128)(2,1)S(1)} all-gather(bf16[16,16,128]{2,1,0:T(8,128)(2,1)S(1)} %pack.1), channel_id=2, replica_groups=mesh['ylo'=2,'xh'=2,'xl'=2,'core'=2,'z'=8,'yhi'=4] {'yhi'}, dimensions={0}, use_global_device_ids=true | all-gather | bytes 327680 | tf_op jit(solution)/shard_map/all_gather | solution.py:213
  39.3 0.7 fusion.2
  39.9 1.3 %broadcast_in_dim.2 = bf16[8,4,8,16,128]{4,3,2,1,0:T(8,128)(2,1)} broadcast(bf16[4,8,16,128]{3,2,1,0:T(8,128)(2,1)S(1)} %get-tuple-element.34), dimensions={1,2,3,4} | broadcast | bytes 1179648 | tf_op jit(solution)/shard_map/broadcast_in_dim | solution.py:215
  41.2 9.1 %all-to-all-start.1 = ((bf16[8,4,8,16,128]{4,3,2,1,0:T(8,128)(2,1)}), bf16[8,4,8,16,128]{4,3,2,1,0:T(8,128)(2,1)S(1)}, u32[]{:S(2)}, u32[]{:S(2)}) async-start(bf16[8,4,8,16,128]{4,3,2,1,0:T(8,128)(2,1)} %broadcast_in_dim.2), calls=%async_computation.1 | async-start | bytes 2097152 | tf_op jit(solution)/shard_map/all_to_all | solution.py:218
  50.4 3.5 %collective-permute-start.2 = (bf16[128,256]{1,0:T(8,128)(2,1)S(1)}, bf16[128,256]{1,0:T(8,128)(2,1)S(1)}, u32[]{:S(2)}, u32[]{:S(2)}) collective-permute-start(bf16[128,256]{1,0:T(8,128)(2,1)S(1)} %get-tuple-element.29), channel_id=1, source_target_pairs={{0,96},{32,64},{64,32},{96,0},{1,97},{33,65},{65,33},{97,1},{2,98}... | collective-permute-start | bytes 196616 | tf_op jit(solution)/shard_map/ppermute | solution.py:224
  53.9 5.2 %collective-permute-start.1 = (bf16[128,256]{1,0:T(8,128)(2,1)S(1)}, bf16[128,256]{1,0:T(8,128)(2,1)S(1)}, u32[]{:S(2)}, u32[]{:S(2)}) collective-permute-start(bf16[128,256]{1,0:T(8,128)(2,1)S(1)} %get-tuple-element.30), channel_id=1, source_target_pairs={{0,64},{32,96},{64,0},{96,32},{1,65},{33,97},{65,1},{97,33},{2,66}... | collective-permute-start | bytes 196616 | tf_op jit(solution)/shard_map/ppermute | solution.py:224
  59.1 1.9 %collective-permute-start = (bf16[128,256]{1,0:T(8,128)(2,1)S(1)}, bf16[128,256]{1,0:T(8,128)(2,1)S(1)}, u32[]{:S(2)}, u32[]{:S(2)}) collective-permute-start(bf16[128,256]{1,0:T(8,128)(2,1)S(1)} %get-tuple-element.31), channel_id=1, source_target_pairs={{0,32},{32,0},{64,96},{96,64},{1,33},{33,1},{65,97},{97,65},{2,34}... | collective-permute-start | bytes 196616 | tf_op jit(solution)/shard_map/ppermute | solution.py:224
  61.2 1.0 collective-permute-done.l1
  62.3 2.2 %copy-done.1 = bf16[4096,512]{1,0:T(8,128)(2,1)S(1)} copy-done((bf16[4096,512]{1,0:T(8,128)(2,1)S(1)}, bf16[4096,512]{1,0:T(8,128)(2,1)}, u32[]{:S(2)}) %copy-start.1) | copy-done | bytes 4194328
  64.5 0.8 choose.1.g_ref
  65.3 11.1 %all-to-all-done.1.m_ref = bf16[8,4,8,16,128]{4,3,2,1,0:T(8,128)(2,1)S(1)} async-done(((bf16[8,4,8,16,128]{4,3,2,1,0:T(8,128)(2,1)}), bf16[8,4,8,16,128]{4,3,2,1,0:T(8,128)(2,1)S(1)}, u32[]{:S(2)}, u32[]{:S(2)}) %all-to-all-start.1) | async-done | bytes 1048608 | tf_op jit(solution)/shard_map/all_to_all | solution.py:218
  76.4 1.2 %upper.1.mine_ref = bf16[2,256,128]{2,1,0:T(8,128)(2,1)S(1)} custom-call(s32[21]{0:T(128)S(1)} %concatenate.6.idx, bf16[8,256,512]{2,1,0:T(8,128)(2,1)S(1)} %choose.1.g_ref, bf16[8,4,8,16,128]{4,3,2,1,0:T(8,128)(2,1)S(1)} %all-to-all-done.1.m_ref), custom_call_target="tpu_custom_call" | custom-call | flops 268435456 | bytes 3145728 | tf_op jit(solution)/shard_map/upper/pallas_call | solution.py:85
  77.6 9.9 %all-gather.2 = bf16[8,256,128]{2,1,0:T(8,128)(2,1)S(1)} all-gather(bf16[2,256,128]{2,1,0:T(8,128)(2,1)S(1)} %upper.1.mine_ref), channel_id=4, replica_groups=mesh['ylo'=2,'xh'=2,'xl'=2,'core'=2,'z'=8,'yhi'=4] {'xl','core'}, dimensions={0}, use_global_device_ids=true | all-gather | bytes 655360 | tf_op jit(solution)/shard_map/all_gather | solution.py:232
  87.6 0.9 cross.1
  88.5 4.7 %all-to-all-start.2 = ((bf16[32,16,128]{2,1,0:T(8,128)(2,1)}), bf16[32,16,128]{2,1,0:T(8,128)(2,1)S(1)}, u32[]{:S(2)}, u32[]{:S(2)}) async-start(bf16[32,16,128]{2,1,0:T(8,128)(2,1)} %bitcast.11), calls=%async_computation.2 | async-start | bytes 262144 | tf_op jit(solution)/shard_map/all_to_all | solution.py:234
  93.2 0.8 copy-done.4
  94.0 0.8 through.1.add_ref
  94.8 0.6 slice_bitcast_fusion
  95.5 9.0 %all-to-all-done.2.parts_ref = bf16[32,16,128]{2,1,0:T(8,128)(2,1)S(1)} async-done(((bf16[32,16,128]{2,1,0:T(8,128)(2,1)}), bf16[32,16,128]{2,1,0:T(8,128)(2,1)S(1)}, u32[]{:S(2)}, u32[]{:S(2)}) %all-to-all-start.2) | async-done | bytes 131104 | tf_op jit(solution)/shard_map/all_to_all | solution.py:234
  104.5 0.6 settle.1
  105.1 1.2 %copy-done.2 = bf16[32,8,16,128]{3,2,1,0:T(8,128)(2,1)S(1)} copy-done((bf16[32,8,16,128]{3,2,1,0:T(8,128)(2,1)S(1)}, bf16[32,8,16,128]{3,2,1,0:T(8,128)(2,1)}, u32[]{:S(2)}) %copy-start.2) | copy-done | bytes 1048600
  106.3 2.0 %lower.1 = bf16[256,256]{1,0:T(8,128)(2,1)} custom-call(s32[21]{0:T(128)S(1)} %concatenate.6.idx, bf16[8,256,512]{2,1,0:T(8,128)(2,1)S(1)} %choose.1.g_ref, bf16[8,4,8,16,128]{4,3,2,1,0:T(8,128)(2,1)S(1)} %bitcast.29, f32[2,256,128]{2,1,0:T(8,128)S(1)} %through.1.add_ref), custom_call_target="tpu_custom_call" | custom-call | flops 268435456 | bytes 3145728 | tf_op jit(solution)/shard_map/lower/pallas_call | solution.py:156
  (21 shorter events, 0.9 us)
Async XLA Ops:
  7.2 1.7 %copy-start = (bf16[16,2048]{1,0:T(8,128)(2,1)S(1)}, bf16[16,2048]{1,0:T(8,128)(2,1)}, u32[]{:S(2)}) copy-start(bf16[16,2048]{1,0:T(8,128)(2,1)} %param.8) | copy-start | bytes 196612
  7.2 43.1 %copy-start.6 = (bf16[128,1024]{1,0:T(8,128)(2,1)S(1)}, bf16[128,1024]{1,0:T(8,128)(2,1)}, u32[]{:S(2)}) copy-start(bf16[128,1024]{1,0:T(8,128)(2,1)} %param.10) | copy-start | bytes 786436
  7.2 55.1 %all-gather.7.cloned.1.call-start = ((), (), s32[]{:S(2)}) async-start(), calls=%async_computation.3 | async-start | bytes 4456448 | tf_op jit(solution)/shard_map/all_gather | solution.py:205
  9.6 16.9 %all-to-all-start = ((bf16[16,16,384]{2,1,0:T(8,128)(2,1)}), bf16[16,16,384]{2,1,0:T(8,128)(2,1)S(1)}, u32[]{:S(2)}, u32[]{:S(2)}) async-start(bf16[16,16,384]{2,1,0:T(8,128)(2,1)} %maximum_bitcast_fusion), calls=%async_computation | async-start | bytes 393216 | tf_op jit(solution)/shard_map/all_to_all | solution.py:210
  41.2 35.2 %all-to-all-start.1 = ((bf16[8,4,8,16,128]{4,3,2,1,0:T(8,128)(2,1)}), bf16[8,4,8,16,128]{4,3,2,1,0:T(8,128)(2,1)S(1)}, u32[]{:S(2)}, u32[]{:S(2)}) async-start(bf16[8,4,8,16,128]{4,3,2,1,0:T(8,128)(2,1)} %broadcast_in_dim.2), calls=%async_computation.1 | async-start | bytes 2097152 | tf_op jit(solution)/shard_map/all_to_all | solution.py:218
  50.2 54.9 %all-gather.9.cloned.1.call-start = ((), (), s32[]{:S(2)}) async-start(), calls=%async_computation.4 | async-start | bytes 1179648 | tf_op jit(solution)/shard_map/all_gather | solution.py:227
  50.4 10.7 %collective-permute-start.2 = (bf16[128,256]{1,0:T(8,128)(2,1)S(1)}, bf16[128,256]{1,0:T(8,128)(2,1)S(1)}, u32[]{:S(2)}, u32[]{:S(2)}) collective-permute-start(bf16[128,256]{1,0:T(8,128)(2,1)S(1)} %get-tuple-element.29), channel_id=1, source_target_pairs={{0,96},{32,64},{64,32},{96,0},{1,97},{33,65},{65,33},{97,1},{2,98}... | collective-permute-start | bytes 196616 | tf_op jit(solution)/shard_map/ppermute | solution.py:224
  53.9 7.3 %collective-permute-start.1 = (bf16[128,256]{1,0:T(8,128)(2,1)S(1)}, bf16[128,256]{1,0:T(8,128)(2,1)S(1)}, u32[]{:S(2)}, u32[]{:S(2)}) collective-permute-start(bf16[128,256]{1,0:T(8,128)(2,1)S(1)} %get-tuple-element.30), channel_id=1, source_target_pairs={{0,64},{32,96},{64,0},{96,32},{1,65},{33,97},{65,1},{97,33},{2,66}... | collective-permute-start | bytes 196616 | tf_op jit(solution)/shard_map/ppermute | solution.py:224
  59.1 3.1 %collective-permute-start = (bf16[128,256]{1,0:T(8,128)(2,1)S(1)}, bf16[128,256]{1,0:T(8,128)(2,1)S(1)}, u32[]{:S(2)}, u32[]{:S(2)}) collective-permute-start(bf16[128,256]{1,0:T(8,128)(2,1)S(1)} %get-tuple-element.31), channel_id=1, source_target_pairs={{0,32},{32,0},{64,96},{96,64},{1,33},{33,1},{65,97},{97,65},{2,34}... | collective-permute-start | bytes 196616 | tf_op jit(solution)/shard_map/ppermute | solution.py:224
  62.3 3.0 %copy-start.3 = (bf16[128,256]{1,0:T(8,128)(2,1)}, bf16[128,256]{1,0:T(8,128)(2,1)S(1)}, u32[]{:S(2)}) copy-start(bf16[128,256]{1,0:T(8,128)(2,1)S(1)} %collective-permute-done.l1) | copy-start | bytes 196612
  62.3 2.2 %copy-start.1 = (bf16[4096,512]{1,0:T(8,128)(2,1)S(1)}, bf16[4096,512]{1,0:T(8,128)(2,1)}, u32[]{:S(2)}) copy-start(bf16[4096,512]{1,0:T(8,128)(2,1)} %all-gather.7.cloned.1.call-done) | copy-start | bytes 12582916
  65.3 39.2 %copy-start.5 = (bf16[16,128]{1,0:T(8,128)(2,1)S(1)}, bf16[16,128]{1,0:T(8,128)(2,1)}, u32[]{:S(2)}) copy-start(bf16[16,128]{1,0:T(8,128)(2,1)} %dinv_ref.1) | copy-start | bytes 12292
  88.5 16.0 %all-to-all-start.2 = ((bf16[32,16,128]{2,1,0:T(8,128)(2,1)}), bf16[32,16,128]{2,1,0:T(8,128)(2,1)S(1)}, u32[]{:S(2)}, u32[]{:S(2)}) async-start(bf16[32,16,128]{2,1,0:T(8,128)(2,1)} %bitcast.11), calls=%async_computation.2 | async-start | bytes 262144 | tf_op jit(solution)/shard_map/all_to_all | solution.py:234
  93.2 0.8 copy-start.4
  105.1 1.2 %copy-start.2 = (bf16[32,8,16,128]{3,2,1,0:T(8,128)(2,1)S(1)}, bf16[32,8,16,128]{3,2,1,0:T(8,128)(2,1)}, u32[]{:S(2)}) copy-start(bf16[32,8,16,128]{3,2,1,0:T(8,128)(2,1)} %all-gather.9.cloned.1.call-done) | copy-start | bytes 3145732
Sparse Core Ops, SparseCore 0:
  10.2 50.8 all-gather.6
  63.7 38.6 all-gather.8

commit v4 on v3

--- a/solution.py
+++ b/solution.py
@@ -119,24 +119,22 @@
 
 def through_kernel(idx, pair_ref, l0, l1, l2, l3, out_ref):
     member = idx[16]
-    for h in range(2):
-        acc = jnp.zeros((256, 128), F32)
-        for m, link in enumerate((l0, l1, l2, l3)):
-            gone = pair_ref[jnp.bitwise_xor(member, m), 0]
-            cols = link[:, h * 128 : (h + 1) * 128]
-            acc += jnp.dot(gone, cols, preferred_element_type=F32)
-        out_ref[h] = acc
+    acc = jnp.zeros((256, 256), F32)
+    for m, link in enumerate((l0, l1, l2, l3)):
+        gone = pair_ref[jnp.bitwise_xor(member, m), 0]
+        acc += jnp.dot(gone, link[...], preferred_element_type=F32)
+    out_ref[...] = acc
 
 
 def through(idx, pairs, links):
     return pl.pallas_call(
         through_kernel,
-        out_shape=jax.ShapeDtypeStruct((2, 256, 128), F32),
+        out_shape=jax.ShapeDtypeStruct((256, 256), F32),
         grid_spec=pltpu.PrefetchScalarGridSpec(
             num_scalar_prefetch=1,
             grid=(1,),
             in_specs=[whole((4, 2, 256, 128))] + [whole((128, 256))] * 4,
-            out_specs=whole((2, 256, 128)),
+            out_specs=whole((256, 256)),
         ),
         compiler_params=params(),
         name="through",
@@ -144,12 +142,12 @@
 
 
 def lower_kernel(idx, g_ref, m_ref, add_ref, out_ref):
-    for h in range(2):
-        acc = add_ref[h]
-        for s in range(4):
-            cols = m_ref[:, :, 2 * s + h].reshape(512, 128)
-            acc += jnp.dot(g_ref[idx[8 + s]], cols, preferred_element_type=F32)
-        out_ref[h * 128 : (h + 1) * 128, :] = (-acc.T).astype(BF16)
+    acc = add_ref[...]
+    for s in range(4):
+        halves = [m_ref[:, :, 2 * s + h].reshape(512, 128) for h in range(2)]
+        cols = jnp.concatenate(halves, axis=1)
+        acc += jnp.dot(g_ref[idx[8 + s]], cols, preferred_element_type=F32)
+    out_ref[...] = (-acc.T).astype(BF16)
 
 
 def lower(idx, g_own, m_two, add):
@@ -162,7 +160,7 @@
             in_specs=[
                 whole((8, 256, 512)),
                 whole((8, 4, 8, 16, 128)),
-                whole((2, 256, 128)),
+                whole((256, 256)),
             ],
             out_specs=whole((256, 256)),
         ),

time: 117 us -> 117 us (level)
  transfers between devices with their start and end apart: 8 -> 8, of which waited for: 5 -> 5; matrix products, arithmetic and copies ran while one was open for 7% -> 8% of each run, Pallas kernels for 4% -> 4%
where the time goes in v4:
time: 117 us; the launch traced here: 115 us
  starting transfers between devices  34.6 us (30%)
  waiting for transfers between devices  23.7 us (20%)
  blocking collectives  22.1 us (19%)
  between operations  14.9 us (13%)
  local copies, waits for them, and re-layouts  9.45 us (8%)
  Pallas kernels  6.65 us (6%)
  other arithmetic  3.45 us (3%)
    all_gather x1, blocking collectives, per_device(): across = lax.all_gather(packed, 'yhi', axis=0, tiled=False)  12.2 us
    all_to_all x1, waiting for transfers between devices, per_device(): m_one = lax.all_to_all(copies, 'z', 0, 0)  11.1 us
    ppermute x3, starting transfers between devices, per_device(): link = lax.ppermute(link, GROUP, [(i, i ^ m) for i in range(4)])  10.6 us
    all_to_all x1, starting transfers between devices, per_device(): mine = lax.all_to_all(slots, ROW, 0, 0)  10.2 us
    all_gather x1, blocking collectives, per_device(): pairs = lax.all_gather(mine_one, GROUP, axis=0, tiled=False)  9.94 us
    all_to_all x1, starting transfers between devices, per_device(): m_one = lax.all_to_all(copies, 'z', 0, 0)  9.06 us
    all_to_all x1, waiting for transfers between devices, per_device(): parts = lax.all_to_all(part.reshape(32, 16, 128), COL, 0, 0)  9 us
    all_to_all x1, starting transfers between devices, per_device(): parts = lax.all_to_all(part.reshape(32, 16, 128), COL, 0, 0)  4.67 us
  transfers between devices with their start and end apart: 8, of which 5 were waited for; matrix products, arithmetic and copies ran while one was open for 8% of the time, Pallas kernels for 4%

profile of v4, /device:TPU:1, one launch (start us, length us, event | category | flops | bytes accessed | tf_op | source)
XLA Modules:
  0.0 114.9 jit_solution(13150003751818308116)
XLA Ops:
  7.2 0.7 all-gather.7.cloned.1.call-update
  7.9 0.9 copy.20
  8.9 0.7 maximum_bitcast_fusion
  9.6 10.2 %all-to-all-start = ((bf16[16,16,384]{2,1,0:T(8,128)(2,1)}), bf16[16,16,384]{2,1,0:T(8,128)(2,1)S(1)}, u32[]{:S(2)}, u32[]{:S(2)}) async-start(bf16[16,16,384]{2,1,0:T(8,128)(2,1)} %maximum_bitcast_fusion), calls=%async_computation | async-start | bytes 393216 | tf_op jit(solution)/shard_map/all_to_all | solution.py:208
  19.8 1.3 %compare_reduce_fusion = (pred[]{:T(512)}, s32[8]{0:T(128)S(1)}) fusion(s32[]{:T(128)S(6)} %select_n.50, s32[4,8]{1,0:T(4,128)} %param.12, s32[]{:T(128)S(6)} %select_n.46), kind=kLoop, calls=%fused_computation.11 | loop fusion | flops 15 | bytes 73 | tf_op jit(solution)/shard_map/reduce_or | solution.py:198
  21.7 0.9 dynamic-slice_reduce_fusion
  22.6 0.7 compare_reduce_fusion.1
  23.3 0.7 iota_reduce_fusion
  24.0 0.8 concatenate.6.idx
  24.8 1.7 %all-to-all-done.x_ref = bf16[16,16,384]{2,1,0:T(8,128)(2,1)S(1)} async-done(((bf16[16,16,384]{2,1,0:T(8,128)(2,1)}), bf16[16,16,384]{2,1,0:T(8,128)(2,1)S(1)}, u32[]{:S(2)}, u32[]{:S(2)}) %all-to-all-start) | async-done | bytes 196640 | tf_op jit(solution)/shard_map/all_to_all | solution.py:208
  27.1 12.2 %all-gather = bf16[64,16,128]{2,1,0:T(8,128)(2,1)S(1)} all-gather(bf16[16,16,128]{2,1,0:T(8,128)(2,1)S(1)} %pack.1), channel_id=2, replica_groups=mesh['ylo'=2,'xh'=2,'xl'=2,'core'=2,'z'=8,'yhi'=4] {'yhi'}, dimensions={0}, use_global_device_ids=true | all-gather | bytes 327680 | tf_op jit(solution)/shard_map/all_gather | solution.py:211
  39.3 0.7 fusion.2
  39.9 1.3 %broadcast_in_dim.2 = bf16[8,4,8,16,128]{4,3,2,1,0:T(8,128)(2,1)} broadcast(bf16[4,8,16,128]{3,2,1,0:T(8,128)(2,1)S(1)} %get-tuple-element.34), dimensions={1,2,3,4} | broadcast | bytes 1179648 | tf_op jit(solution)/shard_map/broadcast_in_dim | solution.py:213
  41.2 9.1 %all-to-all-start.1 = ((bf16[8,4,8,16,128]{4,3,2,1,0:T(8,128)(2,1)}), bf16[8,4,8,16,128]{4,3,2,1,0:T(8,128)(2,1)S(1)}, u32[]{:S(2)}, u32[]{:S(2)}) async-start(bf16[8,4,8,16,128]{4,3,2,1,0:T(8,128)(2,1)} %broadcast_in_dim.2), calls=%async_computation.1 | async-start | bytes 2097152 | tf_op jit(solution)/shard_map/all_to_all | solution.py:216
  50.4 3.5 %collective-permute-start.2 = (bf16[128,256]{1,0:T(8,128)(2,1)S(1)}, bf16[128,256]{1,0:T(8,128)(2,1)S(1)}, u32[]{:S(2)}, u32[]{:S(2)}) collective-permute-start(bf16[128,256]{1,0:T(8,128)(2,1)S(1)} %get-tuple-element.29), channel_id=1, source_target_pairs={{0,96},{32,64},{64,32},{96,0},{1,97},{33,65},{65,33},{97,1},{2,98}... | collective-permute-start | bytes 196616 | tf_op jit(solution)/shard_map/ppermute | solution.py:222
  53.9 5.2 %collective-permute-start.1 = (bf16[128,256]{1,0:T(8,128)(2,1)S(1)}, bf16[128,256]{1,0:T(8,128)(2,1)S(1)}, u32[]{:S(2)}, u32[]{:S(2)}) collective-permute-start(bf16[128,256]{1,0:T(8,128)(2,1)S(1)} %get-tuple-element.30), channel_id=1, source_target_pairs={{0,64},{32,96},{64,0},{96,32},{1,65},{33,97},{65,1},{97,33},{2,66}... | collective-permute-start | bytes 196616 | tf_op jit(solution)/shard_map/ppermute | solution.py:222
  59.1 1.9 %collective-permute-start = (bf16[128,256]{1,0:T(8,128)(2,1)S(1)}, bf16[128,256]{1,0:T(8,128)(2,1)S(1)}, u32[]{:S(2)}, u32[]{:S(2)}) collective-permute-start(bf16[128,256]{1,0:T(8,128)(2,1)S(1)} %get-tuple-element.31), channel_id=1, source_target_pairs={{0,32},{32,0},{64,96},{96,64},{1,33},{33,1},{65,97},{97,65},{2,34}... | collective-permute-start | bytes 196616 | tf_op jit(solution)/shard_map/ppermute | solution.py:222
  61.2 1.0 collective-permute-done.l1
  62.3 2.2 %copy-done.1 = bf16[4096,512]{1,0:T(8,128)(2,1)S(1)} copy-done((bf16[4096,512]{1,0:T(8,128)(2,1)S(1)}, bf16[4096,512]{1,0:T(8,128)(2,1)}, u32[]{:S(2)}) %copy-start.1) | copy-done | bytes 4194328
  64.5 0.8 choose.1.g_ref
  65.3 11.1 %all-to-all-done.1.m_ref = bf16[8,4,8,16,128]{4,3,2,1,0:T(8,128)(2,1)S(1)} async-done(((bf16[8,4,8,16,128]{4,3,2,1,0:T(8,128)(2,1)}), bf16[8,4,8,16,128]{4,3,2,1,0:T(8,128)(2,1)S(1)}, u32[]{:S(2)}, u32[]{:S(2)}) %all-to-all-start.1) | async-done | bytes 1048608 | tf_op jit(solution)/shard_map/all_to_all | solution.py:216
  76.4 1.2 %upper.1.mine_ref = bf16[2,256,128]{2,1,0:T(8,128)(2,1)S(1)} custom-call(s32[21]{0:T(128)S(1)} %concatenate.6.idx, bf16[8,256,512]{2,1,0:T(8,128)(2,1)S(1)} %choose.1.g_ref, bf16[8,4,8,16,128]{4,3,2,1,0:T(8,128)(2,1)S(1)} %all-to-all-done.1.m_ref), custom_call_target="tpu_custom_call" | custom-call | flops 268435456 | bytes 3145728 | tf_op jit(solution)/shard_map/upper/pallas_call | solution.py:85
  77.6 9.9 %all-gather.2 = bf16[8,256,128]{2,1,0:T(8,128)(2,1)S(1)} all-gather(bf16[2,256,128]{2,1,0:T(8,128)(2,1)S(1)} %upper.1.mine_ref), channel_id=4, replica_groups=mesh['ylo'=2,'xh'=2,'xl'=2,'core'=2,'z'=8,'yhi'=4] {'xl','core'}, dimensions={0}, use_global_device_ids=true | all-gather | bytes 655360 | tf_op jit(solution)/shard_map/all_gather | solution.py:230
  87.6 0.9 cross.1
  88.5 4.7 %all-to-all-start.2 = ((bf16[32,16,128]{2,1,0:T(8,128)(2,1)}), bf16[32,16,128]{2,1,0:T(8,128)(2,1)S(1)}, u32[]{:S(2)}, u32[]{:S(2)}) async-start(bf16[32,16,128]{2,1,0:T(8,128)(2,1)} %bitcast.11), calls=%async_computation.2 | async-start | bytes 262144 | tf_op jit(solution)/shard_map/all_to_all | solution.py:232
  93.2 0.8 copy-done.4
  94.0 0.8 through.1.add_ref
  94.8 0.6 slice_bitcast_fusion
  95.5 9.0 %all-to-all-done.2.parts_ref = bf16[32,16,128]{2,1,0:T(8,128)(2,1)S(1)} async-done(((bf16[32,16,128]{2,1,0:T(8,128)(2,1)}), bf16[32,16,128]{2,1,0:T(8,128)(2,1)S(1)}, u32[]{:S(2)}, u32[]{:S(2)}) %all-to-all-start.2) | async-done | bytes 131104 | tf_op jit(solution)/shard_map/all_to_all | solution.py:232
  104.5 0.6 settle.1
  105.1 1.2 %copy-done.2 = bf16[32,8,16,128]{3,2,1,0:T(8,128)(2,1)S(1)} copy-done((bf16[32,8,16,128]{3,2,1,0:T(8,128)(2,1)S(1)}, bf16[32,8,16,128]{3,2,1,0:T(8,128)(2,1)}, u32[]{:S(2)}) %copy-start.2) | copy-done | bytes 1048600
  106.3 1.7 %lower.1 = bf16[256,256]{1,0:T(8,128)(2,1)} custom-call(s32[21]{0:T(128)S(1)} %concatenate.6.idx, bf16[8,256,512]{2,1,0:T(8,128)(2,1)S(1)} %choose.1.g_ref, bf16[8,4,8,16,128]{4,3,2,1,0:T(8,128)(2,1)S(1)} %bitcast.29, f32[256,256]{1,0:T(8,128)S(1)} %through.1.add_ref), custom_call_target="tpu_custom_call" | custom-call | flops 268435456 | bytes 3145728 | tf_op jit(solution)/shard_map/lower/pallas_call | solution.py:154
  (21 shorter events, 0.9 us)
Async XLA Ops:
  7.2 1.7 %copy-start = (bf16[16,2048]{1,0:T(8,128)(2,1)S(1)}, bf16[16,2048]{1,0:T(8,128)(2,1)}, u32[]{:S(2)}) copy-start(bf16[16,2048]{1,0:T(8,128)(2,1)} %param.8) | copy-start | bytes 196612
  7.2 43.1 %copy-start.6 = (bf16[128,1024]{1,0:T(8,128)(2,1)S(1)}, bf16[128,1024]{1,0:T(8,128)(2,1)}, u32[]{:S(2)}) copy-start(bf16[128,1024]{1,0:T(8,128)(2,1)} %param.10) | copy-start | bytes 786436
  7.2 55.1 %all-gather.7.cloned.1.call-start = ((), (), s32[]{:S(2)}) async-start(), calls=%async_computation.3 | async-start | bytes 4456448 | tf_op jit(solution)/shard_map/all_gather | solution.py:203
  9.6 16.9 %all-to-all-start = ((bf16[16,16,384]{2,1,0:T(8,128)(2,1)}), bf16[16,16,384]{2,1,0:T(8,128)(2,1)S(1)}, u32[]{:S(2)}, u32[]{:S(2)}) async-start(bf16[16,16,384]{2,1,0:T(8,128)(2,1)} %maximum_bitcast_fusion), calls=%async_computation | async-start | bytes 393216 | tf_op jit(solution)/shard_map/all_to_all | solution.py:208
  41.2 35.2 %all-to-all-start.1 = ((bf16[8,4,8,16,128]{4,3,2,1,0:T(8,128)(2,1)}), bf16[8,4,8,16,128]{4,3,2,1,0:T(8,128)(2,1)S(1)}, u32[]{:S(2)}, u32[]{:S(2)}) async-start(bf16[8,4,8,16,128]{4,3,2,1,0:T(8,128)(2,1)} %broadcast_in_dim.2), calls=%async_computation.1 | async-start | bytes 2097152 | tf_op jit(solution)/shard_map/all_to_all | solution.py:216
  50.2 54.9 %all-gather.9.cloned.1.call-start = ((), (), s32[]{:S(2)}) async-start(), calls=%async_computation.4 | async-start | bytes 1179648 | tf_op jit(solution)/shard_map/all_gather | solution.py:225
  50.4 10.7 %collective-permute-start.2 = (bf16[128,256]{1,0:T(8,128)(2,1)S(1)}, bf16[128,256]{1,0:T(8,128)(2,1)S(1)}, u32[]{:S(2)}, u32[]{:S(2)}) collective-permute-start(bf16[128,256]{1,0:T(8,128)(2,1)S(1)} %get-tuple-element.29), channel_id=1, source_target_pairs={{0,96},{32,64},{64,32},{96,0},{1,97},{33,65},{65,33},{97,1},{2,98}... | collective-permute-start | bytes 196616 | tf_op jit(solution)/shard_map/ppermute | solution.py:222
  53.9 7.3 %collective-permute-start.1 = (bf16[128,256]{1,0:T(8,128)(2,1)S(1)}, bf16[128,256]{1,0:T(8,128)(2,1)S(1)}, u32[]{:S(2)}, u32[]{:S(2)}) collective-permute-start(bf16[128,256]{1,0:T(8,128)(2,1)S(1)} %get-tuple-element.30), channel_id=1, source_target_pairs={{0,64},{32,96},{64,0},{96,32},{1,65},{33,97},{65,1},{97,33},{2,66}... | collective-permute-start | bytes 196616 | tf_op jit(solution)/shard_map/ppermute | solution.py:222
  59.1 3.1 %collective-permute-start = (bf16[128,256]{1,0:T(8,128)(2,1)S(1)}, bf16[128,256]{1,0:T(8,128)(2,1)S(1)}, u32[]{:S(2)}, u32[]{:S(2)}) collective-permute-start(bf16[128,256]{1,0:T(8,128)(2,1)S(1)} %get-tuple-element.31), channel_id=1, source_target_pairs={{0,32},{32,0},{64,96},{96,64},{1,33},{33,1},{65,97},{97,65},{2,34}... | collective-permute-start | bytes 196616 | tf_op jit(solution)/shard_map/ppermute | solution.py:222
  62.3 3.0 %copy-start.3 = (bf16[128,256]{1,0:T(8,128)(2,1)}, bf16[128,256]{1,0:T(8,128)(2,1)S(1)}, u32[]{:S(2)}) copy-start(bf16[128,256]{1,0:T(8,128)(2,1)S(1)} %collective-permute-done.l1) | copy-start | bytes 196612
  62.3 2.2 %copy-start.1 = (bf16[4096,512]{1,0:T(8,128)(2,1)S(1)}, bf16[4096,512]{1,0:T(8,128)(2,1)}, u32[]{:S(2)}) copy-start(bf16[4096,512]{1,0:T(8,128)(2,1)} %all-gather.7.cloned.1.call-done) | copy-start | bytes 12582916
  65.3 39.2 %copy-start.5 = (bf16[16,128]{1,0:T(8,128)(2,1)S(1)}, bf16[16,128]{1,0:T(8,128)(2,1)}, u32[]{:S(2)}) copy-start(bf16[16,128]{1,0:T(8,128)(2,1)} %dinv_ref.1) | copy-start | bytes 12292
  88.5 16.0 %all-to-all-start.2 = ((bf16[32,16,128]{2,1,0:T(8,128)(2,1)}), bf16[32,16,128]{2,1,0:T(8,128)(2,1)S(1)}, u32[]{:S(2)}, u32[]{:S(2)}) async-start(bf16[32,16,128]{2,1,0:T(8,128)(2,1)} %bitcast.11), calls=%async_computation.2 | async-start | bytes 262144 | tf_op jit(solution)/shard_map/all_to_all | solution.py:232
  93.2 0.8 copy-start.4
  105.1 1.2 %copy-start.2 = (bf16[32,8,16,128]{3,2,1,0:T(8,128)(2,1)S(1)}, bf16[32,8,16,128]{3,2,1,0:T(8,128)(2,1)}, u32[]{:S(2)}) copy-start(bf16[32,8,16,128]{3,2,1,0:T(8,128)(2,1)} %all-gather.9.cloned.1.call-done) | copy-start | bytes 3145732
Sparse Core Ops, SparseCore 0:
  10.2 50.8 all-gather.6
  63.7 38.6 all-gather.8

commit v5 on v4

--- a/solution.py
+++ b/solution.py
@@ -212,8 +212,9 @@
     up_block, down_block = across[:, :8], across[:, 8:]
     copies = jnp.broadcast_to(up_block, (8, 4, 8, 16, 128))
 
-    copies, parent_link = lax.optimization_barrier((copies, parent_link))
     m_one = lax.all_to_all(copies, "z", 0, 0)
+    g_all, down_block, parent_link = lax.optimization_barrier((g_all, down_block, parent_link))
+    m_two = lax.all_gather(down_block, "z", axis=0, tiled=False)
     links = []
     for m in range(4):
         to = jnp.bitwise_xor(member, m)
@@ -221,10 +222,8 @@
         if m:
             link = lax.ppermute(link, GROUP, [(i, i ^ m) for i in range(4)])
         links.append(link)
-    g_all, down_block, *links = lax.optimization_barrier((g_all, down_block, *links))
-    m_two = lax.all_gather(down_block, "z", axis=0, tiled=False)
     g_own = choose(idx, g_all)
-    m_one, g_own = lax.optimization_barrier((m_one, g_own))
+    m_one, g_own, *links = lax.optimization_barrier((m_one, g_own, *links))
 
     mine_one = upper(idx, g_own, m_one)
     pairs = lax.all_gather(mine_one, GROUP, axis=0, tiled=False)

time: 117 us -> 118 us (level)
  waiting for transfers between devices: 23.7 us -> 25.9 us
  starting transfers between devices: 34.6 us -> 33.3 us
  local copies, waits for them, and re-layouts: 9.45 us -> 10.7 us
    all_gather x1, waiting for transfers between devices: 0.01 us -> 10.4 us  [per_device(): g_all = lax.all_gather(ginv_top, ROW, axis=0, tiled=False)]
    all_to_all x1, waiting for transfers between devices: 11.1 us -> 4.07 us  [per_device(): m_one = lax.all_to_all(copies, 'z', 0, 0)]
    ppermute x3, starting transfers between devices: 10.6 us -> 7.85 us  [per_device(): link = lax.ppermute(link, GROUP, [(i, i ^ m) for i in range(4)])]
    all_to_all x1, starting transfers between devices: 4.67 us -> 6.17 us  [per_device(): parts = lax.all_to_all(part.reshape(32, 16, 128), COL, 0, 0)]
    ppermute x3, waiting for transfers between devices: 1.21 us -> 0.01 us  [per_device(): link = lax.ppermute(link, GROUP, [(i, i ^ m) for i in range(4)])]
  transfers between devices with their start and end apart: 8 -> 8, of which waited for: 5 -> 4; matrix products, arithmetic and copies ran while one was open for 8% -> 8% of each run, Pallas kernels for 4% -> 4%
where the time goes in v5:
time: 118 us; the launch traced here: 117 us
  starting transfers between devices  33.3 us (28%)
  waiting for transfers between devices  25.9 us (22%)
  blocking collectives  22.1 us (19%)
  between operations  14.9 us (13%)
  local copies, waits for them, and re-layouts  10.7 us (9%)
  Pallas kernels  6.66 us (6%)
  other arithmetic  3.45 us (3%)
    all_gather x1, blocking collectives, per_device(): across = lax.all_gather(packed, 'yhi', axis=0, tiled=False)  12.2 us
    all_gather x1, waiting for transfers between devices, per_device(): g_all = lax.all_gather(ginv_top, ROW, axis=0, tiled=False)  10.4 us
    all_to_all x1, starting transfers between devices, per_device(): mine = lax.all_to_all(slots, ROW, 0, 0)  10.2 us
    all_gather x1, blocking collectives, per_device(): pairs = lax.all_gather(mine_one, GROUP, axis=0, tiled=False)  9.94 us
    all_to_all x1, starting transfers between devices, per_device(): m_one = lax.all_to_all(copies, 'z', 0, 0)  9.06 us
    all_to_all x1, waiting for transfers between devices, per_device(): parts = lax.all_to_all(part.reshape(32, 16, 128), COL, 0, 0)  9 us
    ppermute x3, starting transfers between devices, per_device(): link = lax.ppermute(link, GROUP, [(i, i ^ m) for i in range(4)])  7.85 us
    all_to_all x1, starting transfers between devices, per_device(): parts = lax.all_to_all(part.reshape(32, 16, 128), COL, 0, 0)  6.17 us
  transfers between devices with their start and end apart: 8, of which 4 were waited for; matrix products, arithmetic and copies ran while one was open for 8% of the time, Pallas kernels for 4%

profile of v5, /device:TPU:1, one launch (start us, length us, event | category | flops | bytes accessed | tf_op | source)
XLA Modules:
  0.0 117.0 jit_solution(9714246272625310211)
XLA Ops:
  7.2 0.7 all-gather.7.cloned.1.call-update
  7.9 0.9 copy.20
  8.9 0.7 maximum_bitcast_fusion
  9.6 10.2 %all-to-all-start = ((bf16[16,16,384]{2,1,0:T(8,128)(2,1)}), bf16[16,16,384]{2,1,0:T(8,128)(2,1)S(1)}, u32[]{:S(2)}, u32[]{:S(2)}) async-start(bf16[16,16,384]{2,1,0:T(8,128)(2,1)} %maximum_bitcast_fusion), calls=%async_computation | async-start | bytes 393216 | tf_op jit(solution)/shard_map/all_to_all | solution.py:208
  19.8 1.3 %compare_reduce_fusion = (pred[]{:T(512)}, s32[8]{0:T(128)S(1)}) fusion(s32[]{:T(128)S(6)} %select_n.50, s32[4,8]{1,0:T(4,128)} %param.12, s32[]{:T(128)S(6)} %select_n.46), kind=kLoop, calls=%fused_computation.11 | loop fusion | flops 15 | bytes 73 | tf_op jit(solution)/shard_map/reduce_or | solution.py:198
  21.7 0.9 dynamic-slice_reduce_fusion
  22.6 0.7 compare_reduce_fusion.1
  23.3 0.7 iota_reduce_fusion
  24.0 0.8 concatenate.6.idx
  24.8 1.7 %all-to-all-done.x_ref = bf16[16,16,384]{2,1,0:T(8,128)(2,1)S(1)} async-done(((bf16[16,16,384]{2,1,0:T(8,128)(2,1)}), bf16[16,16,384]{2,1,0:T(8,128)(2,1)S(1)}, u32[]{:S(2)}, u32[]{:S(2)}) %all-to-all-start) | async-done | bytes 196640 | tf_op jit(solution)/shard_map/all_to_all | solution.py:208
  27.1 12.2 %all-gather = bf16[64,16,128]{2,1,0:T(8,128)(2,1)S(1)} all-gather(bf16[16,16,128]{2,1,0:T(8,128)(2,1)S(1)} %pack.1), channel_id=2, replica_groups=mesh['ylo'=2,'xh'=2,'xl'=2,'core'=2,'z'=8,'yhi'=4] {'yhi'}, dimensions={0}, use_global_device_ids=true | all-gather | bytes 327680 | tf_op jit(solution)/shard_map/all_gather | solution.py:211
  39.3 0.7 fusion.2
  39.9 1.3 %broadcast_in_dim.2 = bf16[8,4,8,16,128]{4,3,2,1,0:T(8,128)(2,1)} broadcast(bf16[4,8,16,128]{3,2,1,0:T(8,128)(2,1)S(1)} %get-tuple-element.32), dimensions={1,2,3,4} | broadcast | bytes 1179648 | tf_op jit(solution)/shard_map/broadcast_in_dim | solution.py:213
  41.2 9.1 %all-to-all-start.1 = ((bf16[8,4,8,16,128]{4,3,2,1,0:T(8,128)(2,1)}), bf16[8,4,8,16,128]{4,3,2,1,0:T(8,128)(2,1)S(1)}, u32[]{:S(2)}, u32[]{:S(2)}) async-start(bf16[8,4,8,16,128]{4,3,2,1,0:T(8,128)(2,1)} %broadcast_in_dim.2), calls=%async_computation.1 | async-start | bytes 2097152 | tf_op jit(solution)/shard_map/all_to_all | solution.py:215
  50.3 10.4 %all-gather.7.cloned.1.call-done = bf16[4096,512]{1,0:T(8,128)(2,1)} async-done(((bf16[256,512]{1,0:T(8,128)(2,1)}), bf16[4096,512]{1,0:T(8,128)(2,1)}) %all-gather.7.cloned.1.call-update) | async-done | bytes 4194320 | tf_op jit(solution)/shard_map/all_gather | solution.py:203
  60.8 0.7 constant_dynamic-slice_fusion
  61.4 2.2 %collective-permute-start = (bf16[128,256]{1,0:T(8,128)(2,1)}, bf16[128,256]{1,0:T(8,128)(2,1)S(1)}, u32[]{:S(2)}, u32[]{:S(2)}) collective-permute-start(bf16[128,256]{1,0:T(8,128)(2,1)} %get-tuple-element.29), channel_id=1, source_target_pairs={{0,32},{32,0},{64,96},{96,64},{1,33},{33,1},{65,97},{97,65},{2,34}... | collective-permute-start | bytes 196616 | tf_op jit(solution)/shard_map/ppermute | solution.py:223
  63.6 2.4 %collective-permute-start.1 = (bf16[128,256]{1,0:T(8,128)(2,1)}, bf16[128,256]{1,0:T(8,128)(2,1)S(1)}, u32[]{:S(2)}, u32[]{:S(2)}) collective-permute-start(bf16[128,256]{1,0:T(8,128)(2,1)} %get-tuple-element.28), channel_id=1, source_target_pairs={{0,64},{32,96},{64,0},{96,32},{1,65},{33,97},{65,1},{97,33},{2,66}... | collective-permute-start | bytes 196616 | tf_op jit(solution)/shard_map/ppermute | solution.py:223
  66.1 3.2 %collective-permute-start.2 = (bf16[128,256]{1,0:T(8,128)(2,1)S(1)}, bf16[128,256]{1,0:T(8,128)(2,1)S(1)}, u32[]{:S(2)}, u32[]{:S(2)}) collective-permute-start(bf16[128,256]{1,0:T(8,128)(2,1)S(1)} %get-tuple-element.27), channel_id=1, source_target_pairs={{0,96},{32,64},{64,32},{96,0},{1,97},{33,65},{65,33},{97,1},{2,98}... | collective-permute-start | bytes 196616 | tf_op jit(solution)/shard_map/ppermute | solution.py:223
  69.3 2.2 %copy-done.1 = bf16[4096,512]{1,0:T(8,128)(2,1)S(1)} copy-done((bf16[4096,512]{1,0:T(8,128)(2,1)S(1)}, bf16[4096,512]{1,0:T(8,128)(2,1)}, u32[]{:S(2)}) %copy-start.1) | copy-done | bytes 4194328
  71.5 0.8 choose.1.g_ref
  72.3 4.1 %all-to-all-done.1.m_ref = bf16[8,4,8,16,128]{4,3,2,1,0:T(8,128)(2,1)S(1)} async-done(((bf16[8,4,8,16,128]{4,3,2,1,0:T(8,128)(2,1)}), bf16[8,4,8,16,128]{4,3,2,1,0:T(8,128)(2,1)S(1)}, u32[]{:S(2)}, u32[]{:S(2)}) %all-to-all-start.1) | async-done | bytes 1048608 | tf_op jit(solution)/shard_map/all_to_all | solution.py:215
  77.0 1.2 %upper.1.mine_ref = bf16[2,256,128]{2,1,0:T(8,128)(2,1)S(1)} custom-call(s32[21]{0:T(128)S(1)} %concatenate.6.idx, bf16[8,256,512]{2,1,0:T(8,128)(2,1)S(1)} %choose.1.g_ref, bf16[8,4,8,16,128]{4,3,2,1,0:T(8,128)(2,1)S(1)} %all-to-all-done.1.m_ref), custom_call_target="tpu_custom_call" | custom-call | flops 268435456 | bytes 3145728 | tf_op jit(solution)/shard_map/upper/pallas_call | solution.py:85
  78.3 9.9 %all-gather.2 = bf16[8,256,128]{2,1,0:T(8,128)(2,1)S(1)} all-gather(bf16[2,256,128]{2,1,0:T(8,128)(2,1)S(1)} %upper.1.mine_ref), channel_id=4, replica_groups=mesh['ylo'=2,'xh'=2,'xl'=2,'core'=2,'z'=8,'yhi'=4] {'xl','core'}, dimensions={0}, use_global_device_ids=true | all-gather | bytes 655360 | tf_op jit(solution)/shard_map/all_gather | solution.py:229
  88.2 0.9 cross.1
  89.1 6.2 %all-to-all-start.2 = ((bf16[32,16,128]{2,1,0:T(8,128)(2,1)}), bf16[32,16,128]{2,1,0:T(8,128)(2,1)S(1)}, u32[]{:S(2)}, u32[]{:S(2)}) async-start(bf16[32,16,128]{2,1,0:T(8,128)(2,1)} %bitcast.11), calls=%async_computation.2 | async-start | bytes 262144 | tf_op jit(solution)/shard_map/all_to_all | solution.py:231
  95.3 0.8 copy-done.4
  96.1 0.8 through.1.add_ref
  97.0 0.6 slice_bitcast_fusion
  97.6 9.0 %all-to-all-done.2.parts_ref = bf16[32,16,128]{2,1,0:T(8,128)(2,1)S(1)} async-done(((bf16[32,16,128]{2,1,0:T(8,128)(2,1)}), bf16[32,16,128]{2,1,0:T(8,128)(2,1)S(1)}, u32[]{:S(2)}, u32[]{:S(2)}) %all-to-all-start.2) | async-done | bytes 131104 | tf_op jit(solution)/shard_map/all_to_all | solution.py:231
  107.2 1.2 %copy-done.2 = bf16[32,8,16,128]{3,2,1,0:T(8,128)(2,1)S(1)} copy-done((bf16[32,8,16,128]{3,2,1,0:T(8,128)(2,1)S(1)}, bf16[32,8,16,128]{3,2,1,0:T(8,128)(2,1)}, u32[]{:S(2)}) %copy-start.2) | copy-done | bytes 1048600
  108.5 1.7 %lower.1 = bf16[256,256]{1,0:T(8,128)(2,1)} custom-call(s32[21]{0:T(128)S(1)} %concatenate.6.idx, bf16[8,256,512]{2,1,0:T(8,128)(2,1)S(1)} %choose.1.g_ref, bf16[8,4,8,16,128]{4,3,2,1,0:T(8,128)(2,1)S(1)} %bitcast.29, f32[256,256]{1,0:T(8,128)S(1)} %through.1.add_ref), custom_call_target="tpu_custom_call" | custom-call | flops 268435456 | bytes 3145728 | tf_op jit(solution)/shard_map/lower/pallas_call | solution.py:154
  (21 shorter events, 2.0 us)
Async XLA Ops:
  7.2 1.7 %copy-start = (bf16[16,2048]{1,0:T(8,128)(2,1)S(1)}, bf16[16,2048]{1,0:T(8,128)(2,1)}, u32[]{:S(2)}) copy-start(bf16[16,2048]{1,0:T(8,128)(2,1)} %param.8) | copy-start | bytes 196612
  7.2 53.6 %copy-start.6 = (bf16[128,1024]{1,0:T(8,128)(2,1)S(1)}, bf16[128,1024]{1,0:T(8,128)(2,1)}, u32[]{:S(2)}) copy-start(bf16[128,1024]{1,0:T(8,128)(2,1)} %param.10) | copy-start | bytes 786436
  7.2 53.5 %all-gather.7.cloned.1.call-start = ((), (), s32[]{:S(2)}) async-start(), calls=%async_computation.3 | async-start | bytes 4456448 | tf_op jit(solution)/shard_map/all_gather | solution.py:203
  9.6 16.9 %all-to-all-start = ((bf16[16,16,384]{2,1,0:T(8,128)(2,1)}), bf16[16,16,384]{2,1,0:T(8,128)(2,1)S(1)}, u32[]{:S(2)}, u32[]{:S(2)}) async-start(bf16[16,16,384]{2,1,0:T(8,128)(2,1)} %maximum_bitcast_fusion), calls=%async_computation | async-start | bytes 393216 | tf_op jit(solution)/shard_map/all_to_all | solution.py:208
  41.2 35.2 %all-to-all-start.1 = ((bf16[8,4,8,16,128]{4,3,2,1,0:T(8,128)(2,1)}), bf16[8,4,8,16,128]{4,3,2,1,0:T(8,128)(2,1)S(1)}, u32[]{:S(2)}, u32[]{:S(2)}) async-start(bf16[8,4,8,16,128]{4,3,2,1,0:T(8,128)(2,1)} %broadcast_in_dim.2), calls=%async_computation.1 | async-start | bytes 2097152 | tf_op jit(solution)/shard_map/all_to_all | solution.py:215
  50.2 57.0 %all-gather.9.cloned.1.call-start = ((), (), s32[]{:S(2)}) async-start(), calls=%async_computation.4 | async-start | bytes 1179648 | tf_op jit(solution)/shard_map/all_gather | solution.py:217
  61.4 14.9 %collective-permute-start = (bf16[128,256]{1,0:T(8,128)(2,1)}, bf16[128,256]{1,0:T(8,128)(2,1)S(1)}, u32[]{:S(2)}, u32[]{:S(2)}) collective-permute-start(bf16[128,256]{1,0:T(8,128)(2,1)} %get-tuple-element.29), channel_id=1, source_target_pairs={{0,32},{32,0},{64,96},{96,64},{1,33},{33,1},{65,97},{97,65},{2,34}... | collective-permute-start | bytes 196616 | tf_op jit(solution)/shard_map/ppermute | solution.py:223
  63.6 12.8 %collective-permute-start.1 = (bf16[128,256]{1,0:T(8,128)(2,1)}, bf16[128,256]{1,0:T(8,128)(2,1)S(1)}, u32[]{:S(2)}, u32[]{:S(2)}) collective-permute-start(bf16[128,256]{1,0:T(8,128)(2,1)} %get-tuple-element.28), channel_id=1, source_target_pairs={{0,64},{32,96},{64,0},{96,32},{1,65},{33,97},{65,1},{97,33},{2,66}... | collective-permute-start | bytes 196616 | tf_op jit(solution)/shard_map/ppermute | solution.py:223
  66.1 10.3 %collective-permute-start.2 = (bf16[128,256]{1,0:T(8,128)(2,1)S(1)}, bf16[128,256]{1,0:T(8,128)(2,1)S(1)}, u32[]{:S(2)}, u32[]{:S(2)}) collective-permute-start(bf16[128,256]{1,0:T(8,128)(2,1)S(1)} %get-tuple-element.27), channel_id=1, source_target_pairs={{0,96},{32,64},{64,32},{96,0},{1,97},{33,65},{65,33},{97,1},{2,98}... | collective-permute-start | bytes 196616 | tf_op jit(solution)/shard_map/ppermute | solution.py:223
  69.3 2.2 %copy-start.1 = (bf16[4096,512]{1,0:T(8,128)(2,1)S(1)}, bf16[4096,512]{1,0:T(8,128)(2,1)}, u32[]{:S(2)}) copy-start(bf16[4096,512]{1,0:T(8,128)(2,1)} %all-gather.7.cloned.1.call-done) | copy-start | bytes 12582916
  72.3 34.3 %copy-start.5 = (bf16[16,128]{1,0:T(8,128)(2,1)S(1)}, bf16[16,128]{1,0:T(8,128)(2,1)}, u32[]{:S(2)}) copy-start(bf16[16,128]{1,0:T(8,128)(2,1)} %dinv_ref.1) | copy-start | bytes 12292
  76.4 0.6 copy-start.3
  89.1 17.5 %all-to-all-start.2 = ((bf16[32,16,128]{2,1,0:T(8,128)(2,1)}), bf16[32,16,128]{2,1,0:T(8,128)(2,1)S(1)}, u32[]{:S(2)}, u32[]{:S(2)}) async-start(bf16[32,16,128]{2,1,0:T(8,128)(2,1)} %bitcast.11), calls=%async_computation.2 | async-start | bytes 262144 | tf_op jit(solution)/shard_map/all_to_all | solution.py:231
  95.3 0.8 copy-start.4
  107.2 1.2 %copy-start.2 = (bf16[32,8,16,128]{3,2,1,0:T(8,128)(2,1)S(1)}, bf16[32,8,16,128]{3,2,1,0:T(8,128)(2,1)}, u32[]{:S(2)}) copy-start(bf16[32,8,16,128]{3,2,1,0:T(8,128)(2,1)} %all-gather.9.cloned.1.call-done) | copy-start | bytes 3145732
Sparse Core Ops, SparseCore 0:
  10.2 50.4 all-gather.6
  63.4 38.0 all-gather.8
